TPU v7x, 256 devices: a whole 4x4x8 slice. The times are simulated.
256 devices in a mesh: segment: 4 (over x), row: 16 (over z, core), col: 4 (over y).
Axes of the slice: x: 4, y: 4, z: 8, core: 2. Of those that a mesh axis runs over, the one named last changes fastest.
Arguments:
- images: bfloat16 [2, 128, 256, 128], P(None, 'row', 'col'), may hold values from -6 to 6
- cotangent: bfloat16 [2, 128, 256, 128], P(None, 'row', 'col'), may hold values from -6 to 6
- weights: bfloat16 [4, 3, 3, 128, 128], P('segment'), may hold values from -0.1875 to 0.1875
- biases: float32 [4, 128], P('segment'), may hold values from -3 to 3
Outputs:
- segment_outputs: bfloat16 [4, 2, 128, 256, 128], P('segment', None, 'row', 'col')
- segment_grads: bfloat16 [4, 2, 128, 256, 128], P('segment', None, 'row', 'col')
- weight_grads: float32 [4, 3, 3, 128, 128], P('segment')
All inputs are finite; a program needn't handle non-finite values.
Results may differ from a plain program's by a relative error of at most 0.02.
The roundings to bfloat16 on the way count: a program that leaves them out, or rounds other values in their place, can miss the bound.
Values may be sent and summed in bfloat16 or wider, within the bound.
A program may use at most 64 MiB of HBM per device.

v0:
```python
import math

import jax
import jax.numpy as jnp
from jax import lax
from jax.sharding import PartitionSpec as P


def with_halo(cells, sides, width):
    for axis, dim in sides:
        count = lax.axis_size(axis)
        ends = count - 1
        head = lax.slice_in_dim(cells, 0, width, axis=dim)
        tail = lax.slice_in_dim(cells, cells.shape[dim] - width, cells.shape[dim], axis=dim)
        cells = jnp.concatenate(
            [
                lax.ppermute(tail, axis, [(i, (i + 1) % count) for i in range(ends)]),
                cells,
                lax.ppermute(head, axis, [((i + 1) % count, i) for i in range(ends)]),
            ],
            axis=dim,
        )
    return cells


def shifted(array, axis, by):
    length = lax.axis_size(axis)
    pairs = [(i, i + by) for i in range(length) if 0 <= i + by < length]
    return lax.ppermute(array, axis, pairs)


def input_border(active):
    return with_halo(active, (("row", 0), ("col", 1)), 1)


def input_border_again(active):
    return with_halo(active, (("row", 0), ("col", 1)), 1)


def grad_border(upstream):
    return with_halo(upstream, (("row", 0), ("col", 1)), 1)


def conv_padded(padded, kernel, height, breadth):
    channels = padded.shape[2]
    total = jnp.zeros((height * breadth, channels), jnp.float32)
    for tap_row in range(3):
        for tap_col in range(3):
            window = padded[tap_row : tap_row + height, tap_col : tap_col + breadth].reshape(
                -1, channels
            )
            total = total + jnp.dot(
                window, kernel[tap_row, tap_col], preferred_element_type=jnp.float32
            )
    return total.reshape(height, breadth, channels)


def back_padded(padded, kernel, height, breadth):
    channels = padded.shape[2]
    total = jnp.zeros((height * breadth, channels), jnp.float32)
    for tap_row in range(3):
        for tap_col in range(3):
            window = padded[
                2 - tap_row : 2 - tap_row + height, 2 - tap_col : 2 - tap_col + breadth
            ].reshape(-1, channels)
            total = total + lax.dot_general(
                window,
                kernel[tap_row, tap_col],
                (((1,), (1,)), ((), ())),
                preferred_element_type=jnp.float32,
            )
    return total.reshape(height, breadth, channels)


def kernel_padded(padded, upstream):
    height, breadth, channels = upstream.shape
    flat_grad = upstream.reshape(-1, channels)
    taps = []
    for tap_row in range(3):
        for tap_col in range(3):
            window = padded[tap_row : tap_row + height, tap_col : tap_col + breadth].reshape(
                -1, channels
            )
            taps.append(
                lax.dot_general(
                    window, flat_grad, (((0,), (0,)), ((), ())), preferred_element_type=jnp.float32
                )
            )
    return jnp.stack(taps).reshape(3, 3, channels, channels)


def put_slot(buffer, value, which_slot, active_now):
    previous = lax.dynamic_index_in_dim(buffer, which_slot, 0, keepdims=False)
    chosen = jnp.where(active_now, value, previous)
    return lax.dynamic_update_index_in_dim(buffer, chosen, which_slot, 0)


def body(images, cotangent, weights, biases):
    segment_count = lax.axis_size("segment")
    segment_at = lax.axis_index("segment")
    micro = images.shape[0]
    height, breadth, channels = (images.shape[1], images.shape[2], images.shape[3])
    norming = 1.0 / math.sqrt(
        micro * height * lax.axis_size("row") * breadth * lax.axis_size("col")
    )
    kernel = weights[0]
    offset = biases[0]
    ticks = micro + segment_count - 1
    strip_zero = jnp.zeros((height, breadth, channels), jnp.bfloat16)
    saved = jnp.zeros((micro, height, breadth, channels), jnp.bfloat16)
    results = jnp.zeros((micro, height, breadth, channels), jnp.bfloat16)
    gradients = jnp.zeros((micro, height, breadth, channels), jnp.bfloat16)
    incoming = strip_zero
    for tick in range(ticks):
        current = jnp.where(segment_at == 0, images[min(tick, micro - 1)], incoming)
        position = tick - segment_at
        active_now = (position >= 0) & (position < micro)
        which_slot = jnp.clip(position, 0, micro - 1)
        active = jnp.maximum(current, jnp.zeros((), current.dtype))
        bordered = input_border(active)
        branch = conv_padded(bordered, kernel, height, breadth) + offset
        following = (current.astype(jnp.float32) + branch).astype(jnp.bfloat16)
        saved = put_slot(saved, current, which_slot, active_now)
        results = put_slot(results, following, which_slot, active_now)
        if tick < ticks - 1:
            incoming = shifted(following, "segment", 1)
    grad_total = jnp.zeros((3, 3, channels, channels), jnp.float32)
    incoming = strip_zero
    for tick in range(ticks):
        upstream = jnp.where(
            segment_at == segment_count - 1, cotangent[min(tick, micro - 1)], incoming
        )
        position = tick - (segment_count - 1 - segment_at)
        active_now = (position >= 0) & (position < micro)
        which_slot = jnp.clip(position, 0, micro - 1)
        before = lax.dynamic_index_in_dim(saved, which_slot, 0, keepdims=False)
        bordered = input_border_again(jnp.maximum(before, jnp.zeros((), before.dtype)))
        grad_term = jnp.where(
            active_now, kernel_padded(bordered, upstream), jnp.zeros((), jnp.float32)
        )
        grad_total = grad_total + grad_term
        spread = back_padded(grad_border(upstream), kernel, height, breadth)
        grad_in = (
            upstream.astype(jnp.float32) + jnp.where(before > 0, spread, jnp.zeros((), jnp.float32))
        ).astype(jnp.bfloat16)
        gradients = put_slot(gradients, grad_in, which_slot, active_now)
        if tick < ticks - 1:
            incoming = shifted(grad_in, "segment", -1)
    grad_total = lax.psum(grad_total, ("row", "col"))
    return (results[None], gradients[None], (grad_total * norming)[None])


def solution(mesh):
    placed = (
        P(None, "row", "col", None),
        P(None, "row", "col", None),
        P("segment", None, None, None, None),
        P("segment", None),
    )
    return jax.shard_map(
        body,
        mesh=mesh,
        in_specs=placed,
        out_specs=(
            P("segment", None, "row", "col", None),
            P("segment", None, "row", "col", None),
            P("segment", None, None, None, None),
        ),
        check_vma=False,
    )
```

profile of v0, /device:TPU:1, one launch (start us, length us, event | category | flops | bytes accessed | tf_op | source)
XLA Modules:
  0.0 476.5 jit_solution(13758139037243001706)
XLA Ops:
  8.2 5.1 %collective-permute-start.1 = (bf16[1,64,128]{2,1,0:T(8,128)(2,1)S(1)}, bf16[1,64,128]{2,1,0:T(8,128)(2,1)S(1)}, u32[]{:S(2)}, u32[]{:S(2)}) collective-permute-start(bf16[1,64,128]{2,1,0:T(8,128)(2,1)S(1)} %get-tuple-element.202), channel_id=1, source_target_pairs={{4,0},{8,4},{12,8},{16,12},{20,16},{24,20},{28,24},{32,28},{36,32}... | collective-permute-start | bytes 49160 | tf_op jit(solution)/shard_map/ppermute | solution.py:19
  15.4 2.4 collective-permute-start.25
  17.8 3.2 collective-permute-start.24
  21.1 3.0 collective-permute-start.2
  26.9 4.6 collective-permute-start.27
  34.3 3.1 collective-permute-start.4
  38.6 2.0 collective-permute-done.4
  40.9 2.4 collective-permute-start.6
  43.3 3.4 collective-permute-start.5
  47.6 3.3 collective-permute-start.7
  52.5 2.8 collective-permute-done.8
  57.1 4.1 collective-permute-start.9
  61.4 2.2 collective-permute-done.9
  63.8 3.1 collective-permute-start.11
  66.9 4.7 collective-permute-start.10
  72.5 3.2 collective-permute-start.12
  77.3 2.9 collective-permute-done.13
  81.9 4.1 collective-permute-start.14
  86.2 2.7 collective-permute-done.14
  90.9 5.5 %collective-permute-start.15 = (bf16[1,64,128]{2,1,0:T(8,128)(2,1)S(1)}, bf16[1,64,128]{2,1,0:T(8,128)(2,1)S(1)}, u32[]{:S(2)}, u32[]{:S(2)}) collective-permute-start(bf16[1,64,128]{2,1,0:T(8,128)(2,1)S(1)} %get-tuple-element.189), channel_id=1, source_target_pairs={{0,4},{4,8},{8,12},{12,16},{16,20},{20,24},{24,28},{28,32},{32,36}... | collective-permute-start | bytes 49160 | tf_op jit(solution)/shard_map/ppermute | solution.py:17
  100.4 2.8 collective-permute-done.18
  105.1 4.1 collective-permute-start.19
  109.4 2.2 collective-permute-done.19
  113.6 6.0 %collective-permute-start.20 = (bf16[1,64,128]{2,1,0:T(8,128)(2,1)S(1)}, bf16[1,64,128]{2,1,0:T(8,128)(2,1)S(1)}, u32[]{:S(2)}, u32[]{:S(2)}) collective-permute-start(bf16[1,64,128]{2,1,0:T(8,128)(2,1)S(1)} %get-tuple-element.185), channel_id=1, source_target_pairs={{0,4},{4,8},{8,12},{12,16},{16,20},{20,24},{24,28},{28,32},{32,36}... | collective-permute-start | bytes 49160 | tf_op jit(solution)/shard_map/ppermute | solution.py:17
  124.4 2.9 collective-permute-done.23
  130.5 4.9 %collective-permute-start.29 = (bf16[1,64,128]{2,1,0:T(8,128)(2,1)S(1)}, bf16[1,64,128]{2,1,0:T(8,128)(2,1)S(1)}, u32[]{:S(2)}, u32[]{:S(2)}) collective-permute-start(bf16[1,64,128]{2,1,0:T(8,128)(2,1)S(1)} %get-tuple-element.177), channel_id=1, source_target_pairs={{0,4},{4,8},{8,12},{12,16},{16,20},{20,24},{24,28},{28,32},{32,36}... | collective-permute-start | bytes 49160 | tf_op jit(solution)/shard_map/ppermute | solution.py:17
  137.6 4.0 collective-permute-start.32
  145.7 5.8 %collective-permute-done.33 = bf16[8,64,128]{2,1,0:T(8,128)(2,1)S(1)} collective-permute-done((bf16[8,64,128]{2,1,0:T(8,128)(2,1)S(1)}, bf16[8,64,128]{2,1,0:T(8,128)(2,1)S(1)}, u32[]{:S(2)}, u32[]{:S(2)}) %collective-permute-start.33) | collective-permute-done | bytes 131104 | tf_op jit(solution)/shard_map/ppermute | solution.py:29
  151.5 2.1 collective-permute-start.35
  153.7 6.1 %collective-permute-start.34 = (bf16[1,64,128]{2,1,0:T(8,128)(2,1)S(1)}, bf16[1,64,128]{2,1,0:T(8,128)(2,1)S(1)}, u32[]{:S(2)}, u32[]{:S(2)}) collective-permute-start(bf16[1,64,128]{2,1,0:T(8,128)(2,1)S(1)} %get-tuple-element.173), channel_id=1, source_target_pairs={{0,4},{4,8},{8,12},{12,16},{16,20},{20,24},{24,28},{28,32},{32,36}... | collective-permute-start | bytes 49160 | tf_op jit(solution)/shard_map/ppermute | solution.py:17
  161.9 4.5 collective-permute-start.37
  170.5 4.3 collective-permute-done.38
  176.7 7.4 %collective-permute-start.39 = (bf16[1,64,128]{2,1,0:T(8,128)(2,1)S(1)}, bf16[1,64,128]{2,1,0:T(8,128)(2,1)S(1)}, u32[]{:S(2)}, u32[]{:S(2)}) collective-permute-start(bf16[1,64,128]{2,1,0:T(8,128)(2,1)S(1)} %get-tuple-element.169), channel_id=1, source_target_pairs={{0,4},{4,8},{8,12},{12,16},{16,20},{20,24},{24,28},{28,32},{32,36}... | collective-permute-start | bytes 49160 | tf_op jit(solution)/shard_map/ppermute | solution.py:17
  186.3 4.4 collective-permute-start.42
  196.7 5.1 %collective-permute-start.64 = (bf16[1,64,128]{2,1,0:T(8,128)(2,1)S(1)}, bf16[1,64,128]{2,1,0:T(8,128)(2,1)S(1)}, u32[]{:S(2)}, u32[]{:S(2)}) collective-permute-start(bf16[1,64,128]{2,1,0:T(8,128)(2,1)S(1)} %get-tuple-element.161), channel_id=1, source_target_pairs={{0,4},{4,8},{8,12},{12,16},{16,20},{20,24},{24,28},{28,32},{32,36}... | collective-permute-start | bytes 49160 | tf_op jit(solution)/shard_map/ppermute | solution.py:17
  203.7 3.6 collective-permute-start.60
  209.4 4.2 collective-permute-start.56
  215.5 3.6 collective-permute-start.52
  221.1 3.6 collective-permute-start.48
  226.1 4.5 collective-permute-start.66
  232.0 4.2 collective-permute-start.62
  237.6 4.0 collective-permute-start.58
  245.1 4.0 collective-permute-start.54
  252.6 4.0 collective-permute-start.50
  261.2 3.0 collective-permute-start.45
  264.2 6.1 %collective-permute-start.44 = (bf16[1,64,128]{2,1,0:T(8,128)(2,1)S(1)}, bf16[1,64,128]{2,1,0:T(8,128)(2,1)S(1)}, u32[]{:S(2)}, u32[]{:S(2)}) collective-permute-start(bf16[1,64,128]{2,1,0:T(8,128)(2,1)S(1)} %get-tuple-element.165), channel_id=1, source_target_pairs={{0,4},{4,8},{8,12},{12,16},{16,20},{20,24},{24,28},{28,32},{32,36}... | collective-permute-start | bytes 49160 | tf_op jit(solution)/shard_map/ppermute | solution.py:17
  274.9 4.3 collective-permute-start.47
  281.8 186.0 %all-reduce.2.cloned.1.call-done = f32[3,3,128,128]{3,2,1,0:T(8,128)} async-done(((f32[3,3,128,128]{3,2,1,0:T(8,128)}), f32[3,3,128,128]{3,2,1,0:T(8,128)}) %all-reduce.2.cloned.1.call-update) | async-done | bytes 589840 | tf_op jit(solution)/shard_map/psum | solution.py:149
  (354 shorter events, 90.0 us)
Async XLA Ops:
  7.2 460.6 %all-reduce.2.cloned.1.call-start = ((), (), s32[]{:S(2)}) async-start(), calls=%async_computation | async-start | bytes 1179648 | tf_op jit(solution)/shard_map/psum | solution.py:149
  8.2 12.8 %collective-permute-start.1 = (bf16[1,64,128]{2,1,0:T(8,128)(2,1)S(1)}, bf16[1,64,128]{2,1,0:T(8,128)(2,1)S(1)}, u32[]{:S(2)}, u32[]{:S(2)}) collective-permute-start(bf16[1,64,128]{2,1,0:T(8,128)(2,1)S(1)} %get-tuple-element.202), channel_id=1, source_target_pairs={{4,0},{8,4},{12,8},{16,12},{20,16},{24,20},{28,24},{32,28},{36,32}... | collective-permute-start | bytes 49160 | tf_op jit(solution)/shard_map/ppermute | solution.py:19
  13.4 7.7 %collective-permute-start = (bf16[1,64,128]{2,1,0:T(8,128)(2,1)S(1)}, bf16[1,64,128]{2,1,0:T(8,128)(2,1)S(1)}, u32[]{:S(2)}, u32[]{:S(2)}) collective-permute-start(bf16[1,64,128]{2,1,0:T(8,128)(2,1)S(1)} %get-tuple-element.201), channel_id=1, source_target_pairs={{0,4},{4,8},{8,12},{12,16},{16,20},{20,24},{24,28},{28,32},{32,36}... | collective-permute-start | bytes 49160 | tf_op jit(solution)/shard_map/ppermute | solution.py:17
  15.4 10.2 %collective-permute-start.25 = (bf16[1,64,128]{2,1,0:T(8,128)(2,1)S(1)}, bf16[1,64,128]{2,1,0:T(8,128)(2,1)S(1)}, u32[]{:S(2)}, u32[]{:S(2)}) collective-permute-start(bf16[1,64,128]{2,1,0:T(8,128)(2,1)S(1)} %get-tuple-element.182), channel_id=1, source_target_pairs={{4,0},{8,4},{12,8},{16,12},{20,16},{24,20},{28,24},{32,28},{36,32}... | collective-permute-start | bytes 49160 | tf_op jit(solution)/shard_map/ppermute | solution.py:19
  17.8 7.8 %collective-permute-start.24 = (bf16[1,64,128]{2,1,0:T(8,128)(2,1)S(1)}, bf16[1,64,128]{2,1,0:T(8,128)(2,1)S(1)}, u32[]{:S(2)}, u32[]{:S(2)}) collective-permute-start(bf16[1,64,128]{2,1,0:T(8,128)(2,1)S(1)} %get-tuple-element.181), channel_id=1, source_target_pairs={{0,4},{4,8},{8,12},{12,16},{16,20},{20,24},{24,28},{28,32},{32,36}... | collective-permute-start | bytes 49160 | tf_op jit(solution)/shard_map/ppermute | solution.py:17
  21.1 10.8 %collective-permute-start.2 = (bf16[10,1,128]{2,1,0:T(2,128)(2,1)S(1)}, bf16[10,1,128]{2,1,0:T(2,128)(2,1)S(1)}, u32[]{:S(2)}, u32[]{:S(2)}) collective-permute-start(bf16[10,1,128]{2,1,0:T(2,128)(2,1)S(1)} %get-tuple-element.151), channel_id=1, source_target_pairs={{0,1},{1,2},{2,3},{4,5},{5,6},{6,7},{8,9},{9,10},{10,11},{12,13},{... | collective-permute-start | bytes 7688 | tf_op jit(solution)/shard_map/ppermute | solution.py:17
  24.1 7.8 %collective-permute-start.3 = (bf16[10,1,128]{2,1,0:T(2,128)(2,1)S(1)}, bf16[10,1,128]{2,1,0:T(2,128)(2,1)S(1)}, u32[]{:S(2)}, u32[]{:S(2)}) collective-permute-start(bf16[10,1,128]{2,1,0:T(2,128)(2,1)S(1)} %get-tuple-element.152), channel_id=1, source_target_pairs={{1,0},{2,1},{3,2},{5,4},{6,5},{7,6},{9,8},{10,9},{11,10},{13,12},{... | collective-permute-start | bytes 7688 | tf_op jit(solution)/shard_map/ppermute | solution.py:19
  25.6 11.9 %collective-permute-start.26 = (bf16[10,1,128]{2,1,0:T(2,128)(2,1)S(1)}, bf16[10,1,128]{2,1,0:T(2,128)(2,1)S(1)}, u32[]{:S(2)}, u32[]{:S(2)}) collective-permute-start(bf16[10,1,128]{2,1,0:T(2,128)(2,1)S(1)} %get-tuple-element.131), channel_id=1, source_target_pairs={{1,0},{2,1},{3,2},{5,4},{6,5},{7,6},{9,8},{10,9},{11,10},{13,12},{... | collective-permute-start | bytes 7688 | tf_op jit(solution)/shard_map/ppermute | solution.py:19
  26.9 10.6 %collective-permute-start.27 = (bf16[10,1,128]{2,1,0:T(2,128)(2,1)S(1)}, bf16[10,1,128]{2,1,0:T(2,128)(2,1)S(1)}, u32[]{:S(2)}, u32[]{:S(2)}) collective-permute-start(bf16[10,1,128]{2,1,0:T(2,128)(2,1)S(1)} %get-tuple-element.132), channel_id=1, source_target_pairs={{0,1},{1,2},{2,3},{4,5},{5,6},{6,7},{8,9},{9,10},{10,11},{12,13},{... | collective-permute-start | bytes 7688 | tf_op jit(solution)/shard_map/ppermute | solution.py:17
  34.3 6.3 %collective-permute-start.4 = (bf16[8,64,128]{2,1,0:T(8,128)(2,1)S(1)}, bf16[8,64,128]{2,1,0:T(8,128)(2,1)S(1)}, u32[]{:S(2)}, u32[]{:S(2)}) collective-permute-start(bf16[8,64,128]{2,1,0:T(8,128)(2,1)S(1)} %fusion.65), channel_id=1, source_target_pairs={{0,64},{64,128},{128,192},{1,65},{65,129},{129,193},{2,66},{66,130... | collective-permute-start | bytes 393224 | tf_op jit(solution)/shard_map/ppermute | solution.py:29
  57.1 6.6 %collective-permute-start.9 = (bf16[8,64,128]{2,1,0:T(8,128)(2,1)S(1)}, bf16[8,64,128]{2,1,0:T(8,128)(2,1)S(1)}, u32[]{:S(2)}, u32[]{:S(2)}) collective-permute-start(bf16[8,64,128]{2,1,0:T(8,128)(2,1)S(1)} %get-tuple-element.22), channel_id=1, source_target_pairs={{0,64},{64,128},{128,192},{1,65},{65,129},{129,193},{2,66},{66,130... | collective-permute-start | bytes 393224 | tf_op jit(solution)/shard_map/ppermute | solution.py:29
  63.8 7.9 %collective-permute-start.11 = (bf16[1,64,128]{2,1,0:T(8,128)(2,1)S(1)}, bf16[1,64,128]{2,1,0:T(8,128)(2,1)S(1)}, u32[]{:S(2)}, u32[]{:S(2)}) collective-permute-start(bf16[1,64,128]{2,1,0:T(8,128)(2,1)S(1)} %get-tuple-element.194), channel_id=1, source_target_pairs={{4,0},{8,4},{12,8},{16,12},{20,16},{24,20},{28,24},{32,28},{36,32}... | collective-permute-start | bytes 49160 | tf_op jit(solution)/shard_map/ppermute | solution.py:19
  81.9 7.0 %collective-permute-start.14 = (bf16[8,64,128]{2,1,0:T(8,128)(2,1)S(1)}, bf16[8,64,128]{2,1,0:T(8,128)(2,1)S(1)}, u32[]{:S(2)}, u32[]{:S(2)}) collective-permute-start(bf16[8,64,128]{2,1,0:T(8,128)(2,1)S(1)} %get-tuple-element.20), channel_id=1, source_target_pairs={{0,64},{64,128},{128,192},{1,65},{65,129},{129,193},{2,66},{66,130... | collective-permute-start | bytes 393224 | tf_op jit(solution)/shard_map/ppermute | solution.py:29
  88.9 7.5 %collective-permute-start.16 = (bf16[1,64,128]{2,1,0:T(8,128)(2,1)S(1)}, bf16[1,64,128]{2,1,0:T(8,128)(2,1)S(1)}, u32[]{:S(2)}, u32[]{:S(2)}) collective-permute-start(bf16[1,64,128]{2,1,0:T(8,128)(2,1)S(1)} %get-tuple-element.190), channel_id=1, source_target_pairs={{4,0},{8,4},{12,8},{16,12},{20,16},{24,20},{28,24},{32,28},{36,32}... | collective-permute-start | bytes 49160 | tf_op jit(solution)/shard_map/ppermute | solution.py:19
  90.9 6.4 %collective-permute-start.15 = (bf16[1,64,128]{2,1,0:T(8,128)(2,1)S(1)}, bf16[1,64,128]{2,1,0:T(8,128)(2,1)S(1)}, u32[]{:S(2)}, u32[]{:S(2)}) collective-permute-start(bf16[1,64,128]{2,1,0:T(8,128)(2,1)S(1)} %get-tuple-element.189), channel_id=1, source_target_pairs={{0,4},{4,8},{8,12},{12,16},{16,20},{20,24},{24,28},{28,32},{32,36}... | collective-permute-start | bytes 49160 | tf_op jit(solution)/shard_map/ppermute | solution.py:17
  105.1 6.5 %collective-permute-start.19 = (bf16[8,64,128]{2,1,0:T(8,128)(2,1)S(1)}, bf16[8,64,128]{2,1,0:T(8,128)(2,1)S(1)}, u32[]{:S(2)}, u32[]{:S(2)}) collective-permute-start(bf16[8,64,128]{2,1,0:T(8,128)(2,1)S(1)} %get-tuple-element.18), channel_id=1, source_target_pairs={{0,64},{64,128},{128,192},{1,65},{65,129},{129,193},{2,66},{66,130... | collective-permute-start | bytes 393224 | tf_op jit(solution)/shard_map/ppermute | solution.py:29
  111.7 9.5 %collective-permute-start.21 = (bf16[1,64,128]{2,1,0:T(8,128)(2,1)S(1)}, bf16[1,64,128]{2,1,0:T(8,128)(2,1)S(1)}, u32[]{:S(2)}, u32[]{:S(2)}) collective-permute-start(bf16[1,64,128]{2,1,0:T(8,128)(2,1)S(1)} %get-tuple-element.186), channel_id=1, source_target_pairs={{4,0},{8,4},{12,8},{16,12},{20,16},{24,20},{28,24},{32,28},{36,32}... | collective-permute-start | bytes 49160 | tf_op jit(solution)/shard_map/ppermute | solution.py:19
  113.6 7.5 %collective-permute-start.20 = (bf16[1,64,128]{2,1,0:T(8,128)(2,1)S(1)}, bf16[1,64,128]{2,1,0:T(8,128)(2,1)S(1)}, u32[]{:S(2)}, u32[]{:S(2)}) collective-permute-start(bf16[1,64,128]{2,1,0:T(8,128)(2,1)S(1)} %get-tuple-element.185), channel_id=1, source_target_pairs={{0,4},{4,8},{8,12},{12,16},{16,20},{20,24},{24,28},{28,32},{32,36}... | collective-permute-start | bytes 49160 | tf_op jit(solution)/shard_map/ppermute | solution.py:17
  119.7 8.9 %collective-permute-start.28 = (bf16[8,64,128]{2,1,0:T(8,128)(2,1)S(1)}, bf16[8,64,128]{2,1,0:T(8,128)(2,1)S(1)}, u32[]{:S(2)}, u32[]{:S(2)}) collective-permute-start(bf16[8,64,128]{2,1,0:T(8,128)(2,1)S(1)} %add_convert_fusion.4), channel_id=1, source_target_pairs={{64,0},{128,64},{192,128},{65,1},{129,65},{193,129},{66,2},{130,66... | collective-permute-start | bytes 393224 | tf_op jit(solution)/shard_map/ppermute | solution.py:29
  128.6 7.0 %collective-permute-start.30 = (bf16[1,64,128]{2,1,0:T(8,128)(2,1)S(1)}, bf16[1,64,128]{2,1,0:T(8,128)(2,1)S(1)}, u32[]{:S(2)}, u32[]{:S(2)}) collective-permute-start(bf16[1,64,128]{2,1,0:T(8,128)(2,1)S(1)} %get-tuple-element.178), channel_id=1, source_target_pairs={{4,0},{8,4},{12,8},{16,12},{20,16},{24,20},{28,24},{32,28},{36,32}... | collective-permute-start | bytes 49160 | tf_op jit(solution)/shard_map/ppermute | solution.py:19
  144.3 7.3 %collective-permute-start.33 = (bf16[8,64,128]{2,1,0:T(8,128)(2,1)S(1)}, bf16[8,64,128]{2,1,0:T(8,128)(2,1)S(1)}, u32[]{:S(2)}, u32[]{:S(2)}) collective-permute-start(bf16[8,64,128]{2,1,0:T(8,128)(2,1)S(1)} %get-tuple-element.8), channel_id=1, source_target_pairs={{64,0},{128,64},{192,128},{65,1},{129,65},{193,129},{66,2},{130,66... | collective-permute-start | bytes 393224 | tf_op jit(solution)/shard_map/ppermute | solution.py:29
  151.5 8.2 %collective-permute-start.35 = (bf16[1,64,128]{2,1,0:T(8,128)(2,1)S(1)}, bf16[1,64,128]{2,1,0:T(8,128)(2,1)S(1)}, u32[]{:S(2)}, u32[]{:S(2)}) collective-permute-start(bf16[1,64,128]{2,1,0:T(8,128)(2,1)S(1)} %get-tuple-element.174), channel_id=1, source_target_pairs={{4,0},{8,4},{12,8},{16,12},{20,16},{24,20},{28,24},{32,28},{36,32}... | collective-permute-start | bytes 49160 | tf_op jit(solution)/shard_map/ppermute | solution.py:19
  153.7 6.9 %collective-permute-start.34 = (bf16[1,64,128]{2,1,0:T(8,128)(2,1)S(1)}, bf16[1,64,128]{2,1,0:T(8,128)(2,1)S(1)}, u32[]{:S(2)}, u32[]{:S(2)}) collective-permute-start(bf16[1,64,128]{2,1,0:T(8,128)(2,1)S(1)} %get-tuple-element.173), channel_id=1, source_target_pairs={{0,4},{4,8},{8,12},{12,16},{16,20},{20,24},{24,28},{28,32},{32,36}... | collective-permute-start | bytes 49160 | tf_op jit(solution)/shard_map/ppermute | solution.py:17
  160.6 6.0 %collective-permute-start.36 = (bf16[10,1,128]{2,1,0:T(2,128)(2,1)S(1)}, bf16[10,1,128]{2,1,0:T(2,128)(2,1)S(1)}, u32[]{:S(2)}, u32[]{:S(2)}) collective-permute-start(bf16[10,1,128]{2,1,0:T(2,128)(2,1)S(1)} %get-tuple-element.123), channel_id=1, source_target_pairs={{1,0},{2,1},{3,2},{5,4},{6,5},{7,6},{9,8},{10,9},{11,10},{13,12},{... | collective-permute-start | bytes 7688 | tf_op jit(solution)/shard_map/ppermute | solution.py:19
  174.8 9.4 %collective-permute-start.40 = (bf16[1,64,128]{2,1,0:T(8,128)(2,1)S(1)}, bf16[1,64,128]{2,1,0:T(8,128)(2,1)S(1)}, u32[]{:S(2)}, u32[]{:S(2)}) collective-permute-start(bf16[1,64,128]{2,1,0:T(8,128)(2,1)S(1)} %get-tuple-element.170), channel_id=1, source_target_pairs={{4,0},{8,4},{12,8},{16,12},{20,16},{24,20},{28,24},{32,28},{36,32}... | collective-permute-start | bytes 49160 | tf_op jit(solution)/shard_map/ppermute | solution.py:19
  176.7 8.3 %collective-permute-start.39 = (bf16[1,64,128]{2,1,0:T(8,128)(2,1)S(1)}, bf16[1,64,128]{2,1,0:T(8,128)(2,1)S(1)}, u32[]{:S(2)}, u32[]{:S(2)}) collective-permute-start(bf16[1,64,128]{2,1,0:T(8,128)(2,1)S(1)} %get-tuple-element.169), channel_id=1, source_target_pairs={{0,4},{4,8},{8,12},{12,16},{16,20},{20,24},{24,28},{28,32},{32,36}... | collective-permute-start | bytes 49160 | tf_op jit(solution)/shard_map/ppermute | solution.py:17
  185.0 6.0 %collective-permute-start.41 = (bf16[10,1,128]{2,1,0:T(2,128)(2,1)S(1)}, bf16[10,1,128]{2,1,0:T(2,128)(2,1)S(1)}, u32[]{:S(2)}, u32[]{:S(2)}) collective-permute-start(bf16[10,1,128]{2,1,0:T(2,128)(2,1)S(1)} %get-tuple-element.119), channel_id=1, source_target_pairs={{1,0},{2,1},{3,2},{5,4},{6,5},{7,6},{9,8},{10,9},{11,10},{13,12},{... | collective-permute-start | bytes 7688 | tf_op jit(solution)/shard_map/ppermute | solution.py:19
  193.4 67.8 %collective-permute-start.43 = (bf16[8,64,128]{2,1,0:T(8,128)(2,1)S(1)}, bf16[8,64,128]{2,1,0:T(8,128)(2,1)S(1)}, u32[]{:S(2)}, u32[]{:S(2)}) collective-permute-start(bf16[8,64,128]{2,1,0:T(8,128)(2,1)S(1)} %get-tuple-element.29), channel_id=1, source_target_pairs={{64,0},{128,64},{192,128},{65,1},{129,65},{193,129},{66,2},{130,66... | collective-permute-start | bytes 393224 | tf_op jit(solution)/shard_map/ppermute | solution.py:29
  194.7 12.7 %collective-permute-start.65 = (bf16[1,64,128]{2,1,0:T(8,128)(2,1)S(1)}, bf16[1,64,128]{2,1,0:T(8,128)(2,1)S(1)}, u32[]{:S(2)}, u32[]{:S(2)}) collective-permute-start(bf16[1,64,128]{2,1,0:T(8,128)(2,1)S(1)} %get-tuple-element.162), channel_id=1, source_target_pairs={{4,0},{8,4},{12,8},{16,12},{20,16},{24,20},{28,24},{32,28},{36,32}... | collective-permute-start | bytes 49160 | tf_op jit(solution)/shard_map/ppermute | solution.py:19
  196.7 12.7 %collective-permute-start.64 = (bf16[1,64,128]{2,1,0:T(8,128)(2,1)S(1)}, bf16[1,64,128]{2,1,0:T(8,128)(2,1)S(1)}, u32[]{:S(2)}, u32[]{:S(2)}) collective-permute-start(bf16[1,64,128]{2,1,0:T(8,128)(2,1)S(1)} %get-tuple-element.161), channel_id=1, source_target_pairs={{0,4},{4,8},{8,12},{12,16},{16,20},{20,24},{24,28},{28,32},{32,36}... | collective-permute-start | bytes 49160 | tf_op jit(solution)/shard_map/ppermute | solution.py:17
  201.8 11.8 %collective-permute-start.61 = (bf16[1,64,128]{2,1,0:T(8,128)(2,1)S(1)}, bf16[1,64,128]{2,1,0:T(8,128)(2,1)S(1)}, u32[]{:S(2)}, u32[]{:S(2)}) collective-permute-start(bf16[1,64,128]{2,1,0:T(8,128)(2,1)S(1)} %get-tuple-element.160), channel_id=1, source_target_pairs={{4,0},{8,4},{12,8},{16,12},{20,16},{24,20},{28,24},{32,28},{36,32}... | collective-permute-start | bytes 49160 | tf_op jit(solution)/shard_map/ppermute | solution.py:19
  203.7 11.8 %collective-permute-start.60 = (bf16[1,64,128]{2,1,0:T(8,128)(2,1)S(1)}, bf16[1,64,128]{2,1,0:T(8,128)(2,1)S(1)}, u32[]{:S(2)}, u32[]{:S(2)}) collective-permute-start(bf16[1,64,128]{2,1,0:T(8,128)(2,1)S(1)} %get-tuple-element.159), channel_id=1, source_target_pairs={{0,4},{4,8},{8,12},{12,16},{16,20},{20,24},{24,28},{28,32},{32,36}... | collective-permute-start | bytes 49160 | tf_op jit(solution)/shard_map/ppermute | solution.py:17
  207.4 11.8 %collective-permute-start.57 = (bf16[1,64,128]{2,1,0:T(8,128)(2,1)S(1)}, bf16[1,64,128]{2,1,0:T(8,128)(2,1)S(1)}, u32[]{:S(2)}, u32[]{:S(2)}) collective-permute-start(bf16[1,64,128]{2,1,0:T(8,128)(2,1)S(1)} %get-tuple-element.158), channel_id=1, source_target_pairs={{4,0},{8,4},{12,8},{16,12},{20,16},{24,20},{28,24},{32,28},{36,32}... | collective-permute-start | bytes 49160 | tf_op jit(solution)/shard_map/ppermute | solution.py:19
  209.4 11.8 %collective-permute-start.56 = (bf16[1,64,128]{2,1,0:T(8,128)(2,1)S(1)}, bf16[1,64,128]{2,1,0:T(8,128)(2,1)S(1)}, u32[]{:S(2)}, u32[]{:S(2)}) collective-permute-start(bf16[1,64,128]{2,1,0:T(8,128)(2,1)S(1)} %get-tuple-element.157), channel_id=1, source_target_pairs={{0,4},{4,8},{8,12},{12,16},{16,20},{20,24},{24,28},{28,32},{32,36}... | collective-permute-start | bytes 49160 | tf_op jit(solution)/shard_map/ppermute | solution.py:17
  213.6 11.2 %collective-permute-start.53 = (bf16[1,64,128]{2,1,0:T(8,128)(2,1)S(1)}, bf16[1,64,128]{2,1,0:T(8,128)(2,1)S(1)}, u32[]{:S(2)}, u32[]{:S(2)}) collective-permute-start(bf16[1,64,128]{2,1,0:T(8,128)(2,1)S(1)} %get-tuple-element.156), channel_id=1, source_target_pairs={{4,0},{8,4},{12,8},{16,12},{20,16},{24,20},{28,24},{32,28},{36,32}... | collective-permute-start | bytes 49160 | tf_op jit(solution)/shard_map/ppermute | solution.py:19
  215.5 10.6 %collective-permute-start.52 = (bf16[1,64,128]{2,1,0:T(8,128)(2,1)S(1)}, bf16[1,64,128]{2,1,0:T(8,128)(2,1)S(1)}, u32[]{:S(2)}, u32[]{:S(2)}) collective-permute-start(bf16[1,64,128]{2,1,0:T(8,128)(2,1)S(1)} %get-tuple-element.155), channel_id=1, source_target_pairs={{0,4},{4,8},{8,12},{12,16},{16,20},{20,24},{24,28},{28,32},{32,36}... | collective-permute-start | bytes 49160 | tf_op jit(solution)/shard_map/ppermute | solution.py:17
  219.2 11.5 %collective-permute-start.49 = (bf16[1,64,128]{2,1,0:T(8,128)(2,1)S(1)}, bf16[1,64,128]{2,1,0:T(8,128)(2,1)S(1)}, u32[]{:S(2)}, u32[]{:S(2)}) collective-permute-start(bf16[1,64,128]{2,1,0:T(8,128)(2,1)S(1)} %get-tuple-element.154), channel_id=1, source_target_pairs={{4,0},{8,4},{12,8},{16,12},{20,16},{24,20},{28,24},{32,28},{36,32}... | collective-permute-start | bytes 49160 | tf_op jit(solution)/shard_map/ppermute | solution.py:19
  221.1 10.9 %collective-permute-start.48 = (bf16[1,64,128]{2,1,0:T(8,128)(2,1)S(1)}, bf16[1,64,128]{2,1,0:T(8,128)(2,1)S(1)}, u32[]{:S(2)}, u32[]{:S(2)}) collective-permute-start(bf16[1,64,128]{2,1,0:T(8,128)(2,1)S(1)} %get-tuple-element.153), channel_id=1, source_target_pairs={{0,4},{4,8},{8,12},{12,16},{16,20},{20,24},{24,28},{28,32},{32,36}... | collective-permute-start | bytes 49160 | tf_op jit(solution)/shard_map/ppermute | solution.py:17
  224.8 36.3 %collective-permute-start.67 = (bf16[10,1,128]{2,1,0:T(2,128)(2,1)S(1)}, bf16[10,1,128]{2,1,0:T(2,128)(2,1)S(1)}, u32[]{:S(2)}, u32[]{:S(2)}) collective-permute-start(bf16[10,1,128]{2,1,0:T(2,128)(2,1)S(1)} %get-tuple-element.111), channel_id=1, source_target_pairs={{1,0},{2,1},{3,2},{5,4},{6,5},{7,6},{9,8},{10,9},{11,10},{13,12},{... | collective-permute-start | bytes 7688 | tf_op jit(solution)/shard_map/ppermute | solution.py:19
  226.1 35.0 %collective-permute-start.66 = (bf16[10,1,128]{2,1,0:T(2,128)(2,1)S(1)}, bf16[10,1,128]{2,1,0:T(2,128)(2,1)S(1)}, u32[]{:S(2)}, u32[]{:S(2)}) collective-permute-start(bf16[10,1,128]{2,1,0:T(2,128)(2,1)S(1)} %get-tuple-element.112), channel_id=1, source_target_pairs={{0,1},{1,2},{2,3},{4,5},{5,6},{6,7},{8,9},{9,10},{10,11},{12,13},{... | collective-permute-start | bytes 7688 | tf_op jit(solution)/shard_map/ppermute | solution.py:17
  236.3 7.5 %collective-permute-start.59 = (bf16[10,1,128]{2,1,0:T(2,128)(2,1)S(1)}, bf16[10,1,128]{2,1,0:T(2,128)(2,1)S(1)}, u32[]{:S(2)}, u32[]{:S(2)}) collective-permute-start(bf16[10,1,128]{2,1,0:T(2,128)(2,1)S(1)} %get-tuple-element.103), channel_id=1, source_target_pairs={{1,0},{2,1},{3,2},{5,4},{6,5},{7,6},{9,8},{10,9},{11,10},{13,12},{... | collective-permute-start | bytes 7688 | tf_op jit(solution)/shard_map/ppermute | solution.py:19
  237.6 7.5 %collective-permute-start.58 = (bf16[10,1,128]{2,1,0:T(2,128)(2,1)S(1)}, bf16[10,1,128]{2,1,0:T(2,128)(2,1)S(1)}, u32[]{:S(2)}, u32[]{:S(2)}) collective-permute-start(bf16[10,1,128]{2,1,0:T(2,128)(2,1)S(1)} %get-tuple-element.104), channel_id=1, source_target_pairs={{0,1},{1,2},{2,3},{4,5},{5,6},{6,7},{8,9},{9,10},{10,11},{12,13},{... | collective-permute-start | bytes 7688 | tf_op jit(solution)/shard_map/ppermute | solution.py:17
  243.8 7.5 %collective-permute-start.55 = (bf16[10,1,128]{2,1,0:T(2,128)(2,1)S(1)}, bf16[10,1,128]{2,1,0:T(2,128)(2,1)S(1)}, u32[]{:S(2)}, u32[]{:S(2)}) collective-permute-start(bf16[10,1,128]{2,1,0:T(2,128)(2,1)S(1)} %get-tuple-element.99), channel_id=1, source_target_pairs={{1,0},{2,1},{3,2},{5,4},{6,5},{7,6},{9,8},{10,9},{11,10},{13,12},{... | collective-permute-start | bytes 7688 | tf_op jit(solution)/shard_map/ppermute | solution.py:19
  245.1 7.5 %collective-permute-start.54 = (bf16[10,1,128]{2,1,0:T(2,128)(2,1)S(1)}, bf16[10,1,128]{2,1,0:T(2,128)(2,1)S(1)}, u32[]{:S(2)}, u32[]{:S(2)}) collective-permute-start(bf16[10,1,128]{2,1,0:T(2,128)(2,1)S(1)} %get-tuple-element.100), channel_id=1, source_target_pairs={{0,1},{1,2},{2,3},{4,5},{5,6},{6,7},{8,9},{9,10},{10,11},{12,13},{... | collective-permute-start | bytes 7688 | tf_op jit(solution)/shard_map/ppermute | solution.py:17
  251.3 7.5 %collective-permute-start.51 = (bf16[10,1,128]{2,1,0:T(2,128)(2,1)S(1)}, bf16[10,1,128]{2,1,0:T(2,128)(2,1)S(1)}, u32[]{:S(2)}, u32[]{:S(2)}) collective-permute-start(bf16[10,1,128]{2,1,0:T(2,128)(2,1)S(1)} %get-tuple-element.95), channel_id=1, source_target_pairs={{1,0},{2,1},{3,2},{5,4},{6,5},{7,6},{9,8},{10,9},{11,10},{13,12},{... | collective-permute-start | bytes 7688 | tf_op jit(solution)/shard_map/ppermute | solution.py:19
  252.6 6.2 %collective-permute-start.50 = (bf16[10,1,128]{2,1,0:T(2,128)(2,1)S(1)}, bf16[10,1,128]{2,1,0:T(2,128)(2,1)S(1)}, u32[]{:S(2)}, u32[]{:S(2)}) collective-permute-start(bf16[10,1,128]{2,1,0:T(2,128)(2,1)S(1)} %get-tuple-element.96), channel_id=1, source_target_pairs={{0,1},{1,2},{2,3},{4,5},{5,6},{6,7},{8,9},{9,10},{10,11},{12,13},{... | collective-permute-start | bytes 7688 | tf_op jit(solution)/shard_map/ppermute | solution.py:17
  261.2 12.3 %collective-permute-start.45 = (bf16[1,64,128]{2,1,0:T(8,128)(2,1)S(1)}, bf16[1,64,128]{2,1,0:T(8,128)(2,1)S(1)}, u32[]{:S(2)}, u32[]{:S(2)}) collective-permute-start(bf16[1,64,128]{2,1,0:T(8,128)(2,1)S(1)} %get-tuple-element.166), channel_id=1, source_target_pairs={{4,0},{8,4},{12,8},{16,12},{20,16},{24,20},{28,24},{32,28},{36,32}... | collective-permute-start | bytes 49160 | tf_op jit(solution)/shard_map/ppermute | solution.py:19
  264.2 9.3 %collective-permute-start.44 = (bf16[1,64,128]{2,1,0:T(8,128)(2,1)S(1)}, bf16[1,64,128]{2,1,0:T(8,128)(2,1)S(1)}, u32[]{:S(2)}, u32[]{:S(2)}) collective-permute-start(bf16[1,64,128]{2,1,0:T(8,128)(2,1)S(1)} %get-tuple-element.165), channel_id=1, source_target_pairs={{0,4},{4,8},{8,12},{12,16},{16,20},{20,24},{24,28},{28,32},{32,36}... | collective-permute-start | bytes 49160 | tf_op jit(solution)/shard_map/ppermute | solution.py:17
  (27 other events, 321.0 us)
Sparse Core Ops, SparseCore 0:
  273.7 194.0 all-reduce.1
where the time goes:
time: 479 us; the launch traced here: 477 us
  waiting for transfers between devices  223 us (47%)
  starting transfers between devices  200 us (42%)
  matrix products  26.3 us (5%)
  between operations  16.9 us (4%)
  other arithmetic  6.37 us (1%)
    psum x1, waiting for transfers between devices, body(): grad_total = lax.psum(grad_total, ('row', 'col'))  186 us
    ppermute x30, starting transfers between devices, with_halo(): lax.ppermute(tail, axis, [(i, (i + 1) % count) for i in range(ends)])  125 us
    ppermute x30, starting transfers between devices, with_halo(): lax.ppermute(head, axis, [((i + 1) % count, i) for i in range(ends)])  55 us
    ppermute x8, starting transfers between devices, shifted(): return lax.ppermute(array, axis, pairs)  20.6 us
    ppermute x8, waiting for transfers between devices, shifted(): return lax.ppermute(array, axis, pairs)  19.2 us
    ppermute x30, waiting for transfers between devices, with_halo(): lax.ppermute(head, axis, [((i + 1) % count, i) for i in range(ends)])  11.5 us
    dot_general x45, matrix products, kernel_padded(): lax.dot_general(window, flat_grad, (((0,), (0,)), ((), ())), preferred_el...  10.3 us
  transfers between devices with their start and end apart: 69, of which 21 were waited for; matrix products, arithmetic and copies ran while one was open for 4% of the time, Pallas kernels for 0%

commit v1 on v0

v1 whole, which is shorter than its diff:
```python
import functools
import math

import jax
import jax.numpy as jnp
from jax import lax
from jax.experimental import pallas as pl
from jax.experimental.pallas import tpu as pltpu
from jax.sharding import PartitionSpec as P

MESH = pl.DeviceIdType.MESH
BF = jnp.bfloat16
F32 = jnp.float32
SEG, MB, TAPS = 4, 2, 9
REACH = 6
GREACH = 4
SIDE = 16
PAD = 8
DIRS = ((0, 1), (0, -1), (1, 0), (-1, 0), (1, 1), (1, -1), (-1, 1), (-1, -1))


def body_kernel(
    dims, images, cot, w, b, ox, og, ow,
    xin, gin, wall, ball, aa, xs, gg, gs, gm, wf, wb, oxb, ogb, owb,
    dw, s_core, r_core, d_half, s_col, r_col, s_row, r_row, full,
    ss, rs, ls,
):
    rows, width, chan, nrow, ncol, scale = dims
    nz = nrow // 2
    hi = REACH + rows
    tall = rows + 2 * REACH
    wp = width + 2 * PAD
    half, strip = chan // 2, chan // 2 // ncol
    seg, row, col = lax.axis_index("segment"), lax.axis_index("row"), lax.axis_index("col")
    core, z = lax.rem(row, 2), lax.div(row, 2)
    sib = row + 1 - 2 * core

    counter = [0]

    def fresh():
        counter[0] += 1
        return counter[0] - 1

    def remote(src, dst, dev, i):
        return pltpu.make_async_remote_copy(
            src_ref=src, dst_ref=dst, send_sem=ss.at[i], recv_sem=rs.at[i],
            device_id=dev, device_id_type=MESH,
        )

    mine = [
        pltpu.make_async_copy(images.at[m], xin.at[m, pl.ds(REACH, rows), pl.ds(SIDE, width)], ls.at[m])
        for m in range(MB)
    ]
    mine_g = pltpu.make_async_copy(cot, gin.at[:, pl.ds(GREACH, rows), pl.ds(SIDE, width)], ls.at[2])
    mine_w = pltpu.make_async_copy(w, wall.at[seg], ls.at[3])
    mine_b = pltpu.make_async_copy(b, ball.at[seg], ls.at[4])
    for copy in (*mine, mine_g, mine_w, mine_b):
        copy.start()

    barrier = pltpu.get_barrier_semaphore()

    def greet(s, r, c):
        pl.semaphore_signal(barrier, inc=1, device_id=(s, r, c), device_id_type=MESH)

    def inside(dr, dc):
        ok = jnp.bool_(True)
        if dr:
            ok = ok & (row + dr >= 0) & (row + dr < nrow)
        if dc:
            ok = ok & (col + dc >= 0) & (col + dc < ncol)
        return ok

    for k in range(1, SEG):
        greet(lax.rem(seg + k, SEG), row, col)
    for k in range(1, ncol):
        greet(seg, row, lax.rem(col + k, ncol))
    for k in range(1, nz):
        greet(seg, lax.rem(row + 2 * k, nrow), col)
    met = SEG - 1 + ncol - 1 + nz - 1
    for dr, dc in DIRS:
        if dr:
            pl.when(inside(dr, dc))(functools.partial(greet, seg, row + dr, col + dc))
            met = met + inside(dr, dc).astype(jnp.int32)
    pl.semaphore_wait(barrier, met)

    def edges(source, target, reach):
        copies = []
        src_r = {1: (rows - reach, reach), -1: (0, reach), 0: (0, rows)}
        dst_r = {1: (0, reach), -1: (reach + rows, reach), 0: (reach, rows)}
        src_c = {1: (width - SIDE, SIDE), -1: (0, SIDE), 0: (0, width)}
        dst_c = {1: (0, SIDE), -1: (SIDE + width, SIDE), 0: (SIDE, width)}
        for dr, dc in DIRS:
            copies.append((
                remote(
                    source(pl.ds(*src_r[dr]), pl.ds(*src_c[dc])),
                    target(pl.ds(*dst_r[dr]), pl.ds(*dst_c[dc])),
                    (seg, row + dr, col + dc), fresh(),
                ),
                inside(dr, dc), inside(-dr, -dc),
            ))
        return copies

    def start_edges(copies):
        for copy, to, _ in copies:
            pl.when(to)(copy.start)

    def wait_edges(copies):
        for copy, _, of in copies:
            pl.when(of)(copy.wait_recv)

    x_edges = [
        edges(lambda r, c, m=m: images.at[m, r, c], lambda r, c, m=m: xin.at[m, r, c], REACH)
        for m in range(MB)
    ]
    g_edges = edges(lambda r, c: cot.at[:, r, c], lambda r, c: gin.at[:, r, c], GREACH)

    nxt, prv, far = lax.rem(seg + 1, SEG), lax.rem(seg + SEG - 1, SEG), lax.rem(seg + 2, SEG)
    own_rows = pl.ds(pl.multiple_of(half * core, half), half)
    first_q = pl.ds(pl.multiple_of(half * core, half), half // 2)
    second_q = pl.ds(pl.multiple_of(half * core + half // 2, half // 2), half // 2)
    sib_rows = pl.ds(pl.multiple_of(half * (1 - core), half), half)
    up, down = (nxt, row, col), (prv, row, col)
    beside = (seg, sib, col)
    i_up, i_down = fresh(), fresh()
    w_up = remote(w.at[:, own_rows], wall.at[seg, :, own_rows], up, i_up)
    w_down = remote(w.at[:, own_rows], wall.at[seg, :, own_rows], down, i_down)
    got_prv = remote(w.at[:, own_rows], wall.at[prv, :, own_rows], up, i_up)
    got_nxt = remote(w.at[:, own_rows], wall.at[nxt, :, own_rows], down, i_down)

    def onward(which, part, dev, i):
        return remote(wall.at[which, :, part], wall.at[which, :, part], dev, i)

    i_rup, i_rdown, i_s1, i_s2, i_s3 = fresh(), fresh(), fresh(), fresh(), fresh()
    relay_up, relay_down = onward(prv, first_q, up, i_rup), onward(nxt, second_q, down, i_rdown)
    got_rup, got_rdown = onward(far, first_q, up, i_rup), onward(far, second_q, down, i_rdown)
    share_prv, share_nxt = onward(prv, own_rows, beside, i_s1), onward(nxt, own_rows, beside, i_s2)
    share_far = onward(far, own_rows, beside, i_s3)
    got_s1, got_s2 = onward(prv, sib_rows, beside, i_s1), onward(nxt, sib_rows, beside, i_s2)
    got_s3 = onward(far, sib_rows, beside, i_s3)
    b_out, b_in = [], []
    for k in range(1, SEG):
        i = fresh()
        b_out.append(remote(b, ball.at[seg], (lax.rem(seg + k, SEG), row, col), i))
        b_in.append(remote(b, ball.at[lax.rem(seg + SEG - k, SEG)], (lax.rem(seg + k, SEG), row, col), i))

    w_up.start()
    w_down.start()
    start_edges(x_edges[0])
    for copy in b_out:
        copy.start()
    start_edges(x_edges[1])
    start_edges(g_edges)

    got_prv.wait_recv()
    relay_up.start()
    share_prv.start()
    got_nxt.wait_recv()
    relay_down.start()
    share_nxt.start()

    def pass_far():
        got_rup.wait_recv()
        got_rdown.wait_recv()
        share_far.start()

    pl.when(seg == 2)(pass_far)

    def in_image(first, step, count):
        shape = (count, wp, chan)
        r = row * rows - REACH + first + step * lax.broadcasted_iota(jnp.int32, shape, 0)
        c = col * width - PAD + lax.broadcasted_iota(jnp.int32, shape, 1)
        return (r >= 0) & (r < nrow * rows) & (c >= 0) & (c < ncol * width)

    def trio(value):
        flat = value.reshape(-1, chan)
        n = flat.shape[0]
        return [
            v.astype(BF).reshape(value.shape)
            for v in (pltpu.roll(flat, 1, 0), flat, pltpu.roll(flat, n - 1, 0))
        ]

    def take_in(m):
        v = xin[m].astype(F32)[:, PAD : PAD + wp]
        v = jnp.where(in_image(0, 1, tall), v, 0.0)
        xs[m] = v.astype(BF).reshape(tall // 2, 2, wp, chan)
        for t, part in enumerate(trio(jnp.maximum(v, 0.0))):
            aa[0, m, :, :, :, pl.ds(t * chan, chan)] = part.reshape(tall // 2, 2, wp, chan)

    for m in range(MB):
        mine[m].wait()
        wait_edges(x_edges[m])
        take_in(m)

    def build(k):
        zero = jnp.zeros((3 * chan, chan), BF)
        for a in range(4):
            for h in range(2):
                ok = 0 <= a - h <= 2
                block = wall[k, 3 * (a - h) : 3 * (a - h) + 3].reshape(3 * chan, chan) if ok else zero
                wf[k, pl.ds(a * 3 * chan, 3 * chan), pl.ds(h * chan, chan)] = block
                for t in range(3):
                    p = h + 2 - a
                    tile = wall[k, 3 * p + 2 - t] if 0 <= p <= 2 else zero[:chan]
                    wb[k, pl.ds(h * chan, chan), pl.ds((3 * a + t) * chan, chan)] = tile

    def windows(ref, start, count):
        parts = []
        for a in range(4):
            r = start - 1 + a
            parts.append(ref[r // 2 : r // 2 + count // 2, r % 2].reshape(-1, 3 * chan))
        return jnp.concatenate(parts, axis=1)

    def forward(s, m):
        start, count = (s + 1, tall - 2 * (s + 1)) if s < SEG - 1 else (REACH, rows)
        y = jnp.dot(windows(aa.at[s, m], start, count), wf[s], preferred_element_type=F32)
        for h in range(2):
            i, par = (start + h) // 2, (start + h) % 2
            n = count // 2
            x = xs[m, i : i + n, par].astype(F32)
            x = x + (y[:, h * chan : (h + 1) * chan].reshape(n, wp, chan) + ball[s][None])
            x = jnp.where(in_image(start + h, 2, n), x, 0.0).astype(BF)
            xs[m, i : i + n, par] = x
            if s < SEG - 1:
                for t, part in enumerate(trio(jnp.maximum(x.astype(F32), 0.0))):
                    aa[s + 1, m, i : i + n, par, :, pl.ds(t * chan, chan)] = part

    def block_of(ref, m):
        lo, up_to = REACH // 2, hi // 2
        return ref[m, lo:up_to].reshape(rows, wp, chan).astype(F32)

    x_done = pltpu.make_async_copy(oxb, ox, ls.at[5])
    g_done = pltpu.make_async_copy(ogb, og, ls.at[6])

    def emit_x():
        for m in range(MB):
            oxb[m] = block_of(xs, m)[:, PAD : PAD + width].astype(BF)
        x_done.start()

    def emit_g():
        for m in range(MB):
            ogb[m] = block_of(gs, m)[:, PAD : PAD + width].astype(BF)
        g_done.start()

    mine_w.wait()
    mine_b.wait()
    for copy in b_in:
        copy.wait_recv()
    got_s1.wait_recv()
    got_s2.wait_recv()
    pl.when(seg == 2)(got_s3.wait_recv)
    build(0)
    forward(0, 0)
    pl.when(seg != 2)(pass_far)
    forward(0, 1)
    pl.when(seg == 0)(emit_x)
    pl.when(seg != 2)(got_s3.wait_recv)
    for s in range(1, SEG - 1):
        build(s)
        for m in range(MB):
            forward(s, m)
        pl.when(seg == s)(emit_x)
    build(SEG - 1)

    def last():
        for m in range(MB):
            forward(SEG - 1, m)
        emit_x()

    pl.when(seg == SEG - 1)(last)

    mine_g.wait()
    wait_edges(g_edges)
    edge = REACH - GREACH
    for m in range(MB):
        v = gin[m].astype(F32)[:, PAD : PAD + wp]
        v = jnp.where(in_image(edge, 1, tall - 2 * edge), v, 0.0)
        lo, n = edge // 2, tall // 2 - edge
        gs[m, lo : lo + n] = v.astype(BF).reshape(n, 2, wp, chan)
        for t, part in enumerate(trio(v)):
            gg[1, m, lo : lo + n, :, :, pl.ds(t * chan, chan)] = part.reshape(n, 2, wp, chan)
        nothing = jnp.zeros((2, wp, chan), BF)
        gm[m, 0:2] = nothing
        gm[m, rows + 2 : rows + 4] = nothing

    def keep():
        c = lax.broadcasted_iota(jnp.int32, (rows, wp, chan), 1)
        for m in range(MB):
            v = jnp.where((c >= PAD) & (c < PAD + width), block_of(gs, m), 0.0)
            gm[m, 2 : rows + 2] = v.astype(BF)

    def backward(k, m):
        start, count = REACH - k, rows + 2 * k
        y = lax.dot_general(
            windows(gg.at[k % 2, m], start, count), wb[k], (((1,), (1,)), ((), ())),
            preferred_element_type=F32,
        )
        for h in range(2):
            i, par = (start + h) // 2, (start + h) % 2
            n = count // 2
            on = aa[k, m, i : i + n, par, :, pl.ds(chan, chan)].astype(F32) > 0.0
            g = gs[m, i : i + n, par].astype(F32)
            g = (g + jnp.where(on, y[:, h * chan : (h + 1) * chan].reshape(n, wp, chan), 0.0)).astype(BF)
            gs[m, i : i + n, par] = g
            if k:
                for t, part in enumerate(trio(g.astype(F32))):
                    gg[(k - 1) % 2, m, i : i + n, par, :, pl.ds(t * chan, chan)] = part

    for k in range(SEG - 1, 0, -1):
        pl.when(seg == k)(keep)

        def stage(k=k):
            for m in range(MB):
                backward(k, m)

        pl.when(seg <= k)(stage)
        pl.when(seg == k)(emit_g)
    pl.when(seg == 0)(keep)

    total = None
    for m in range(MB):
        lo, up_to = REACH // 2 - 1, hi // 2 + 1
        act = aa[seg, m, lo:up_to].reshape(rows + 4, wp, 3 * chan)[1 : rows + 3].reshape(-1, 3 * chan)
        grads = jnp.concatenate(
            [gm[m, 1 - p : rows + 3 - p].reshape(-1, chan) for p in (-1, 0, 1)], axis=1
        )
        term = lax.dot_general(act, grads, (((0,), (0,)), ((), ())), preferred_element_type=F32)
        total = term if total is None else total + term
    for p in range(3):
        for q in range(3):
            dw[3 * p + q] = total[q * chan : (q + 1) * chan, p * chan : (p + 1) * chan]

    def exchange(pairs):
        for copy, _ in pairs:
            copy.start()
        return pairs

    def arrived(pairs):
        for _, copy in pairs:
            copy.wait_recv()

    late = []
    s_core[...] = dw[:, sib_rows].astype(BF)
    i = fresh()
    core_sum = exchange([(remote(s_core, r_core, beside, i),) * 2])
    late += core_sum
    pl.when(seg == 0)(lambda: backward(0, 0))
    arrived(core_sum)
    d_half[...] = dw[:, own_rows] + r_core[...].astype(F32)
    s_col[...] = d_half[...].astype(BF)
    my_strip = pl.ds(pl.multiple_of(strip * col, strip), strip)
    col_sum = []
    for k in range(1, ncol):
        to = lax.rem(col + k, ncol)
        copy = remote(
            s_col.at[:, pl.ds(pl.multiple_of(strip * to, strip), strip)], r_col.at[k - 1],
            (seg, row, to), fresh(),
        )
        col_sum.append((copy, copy))
    exchange(col_sum)
    late += col_sum

    def final_g():
        backward(0, 1)
        emit_g()

    pl.when(seg == 0)(final_g)
    arrived(col_sum)
    part = d_half[:, my_strip]
    for k in range(1, ncol):
        part = part + r_col[k - 1].astype(F32)
    part = part.astype(BF)
    share = (TAPS - 1) // nz
    for to in range(nz):
        s_row[to, 0:share] = part[to * share : (to + 1) * share]
        s_row[to, share : share + 1] = part[TAPS - 1 :]
    r_row[z] = s_row[z]
    row_sum = []
    for k in range(1, nz):
        to, of = lax.rem(z + k, nz), lax.rem(z + nz - k, nz)
        dev, i = (seg, 2 * to + core, col), fresh()
        row_sum.append((
            remote(s_row.at[to], r_row.at[z], dev, i), remote(s_row.at[to], r_row.at[of], dev, i)
        ))
    exchange(row_sum)
    late += row_sum
    arrived(row_sum)
    done = r_row[0].astype(F32)
    for k in range(1, nz):
        done = done + r_row[k].astype(F32)
    done = (done * scale).astype(BF)
    place = pl.ds(pl.multiple_of(half * core + strip * col, strip), strip)
    full[pl.ds(z * share, share), place] = done[:share]
    full[TAPS - 1 :, place] = done[share:]

    def spread(part_of):
        return full.at[pl.ds(part_of * share, share), place]

    row_all = []
    for k in range(1, nz):
        to, of = lax.rem(z + k, nz), lax.rem(z + nz - k, nz)
        dev, i = (seg, 2 * to + core, col), fresh()
        row_all.append((remote(spread(z), spread(z), dev, i), remote(spread(z), spread(of), dev, i)))
    exchange(row_all)
    late += row_all
    arrived(row_all)

    def column(c):
        return full.at[:, pl.ds(pl.multiple_of(half * core + strip * c, strip), strip)]

    col_all = []
    for k in range(1, ncol):
        to, of = lax.rem(col + k, ncol), lax.rem(col + ncol - k, ncol)
        dev, i = (seg, row, to), fresh()
        col_all.append((remote(column(col), column(col), dev, i), remote(column(col), column(of), dev, i)))
    exchange(col_all)
    late += col_all
    arrived(col_all)
    i = fresh()
    core_all = exchange([(
        remote(full.at[:, own_rows], full.at[:, own_rows], beside, i),
        remote(full.at[:, own_rows], full.at[:, sib_rows], beside, i),
    )])
    late += core_all
    owb[:, own_rows] = full[:, own_rows].astype(F32)
    out_own = pltpu.make_async_copy(owb.at[:, own_rows], ow.at[:, own_rows], ls.at[7])
    out_own.start()

    for copies in (*x_edges, g_edges):
        for copy, to, _ in copies:
            pl.when(to)(copy.wait_send)
    for copy in (w_up, w_down, relay_up, relay_down, share_prv, share_nxt, share_far, *b_out):
        copy.wait_send()
    arrived(core_all)
    owb[:, sib_rows] = full[:, sib_rows].astype(F32)
    out_sib = pltpu.make_async_copy(owb.at[:, sib_rows], ow.at[:, sib_rows], ls.at[8])
    out_sib.start()
    for copy, _ in late:
        copy.wait_send()
    x_done.wait()
    g_done.wait()
    out_own.wait()
    out_sib.wait()


def body(images, cotangent, weights, biases):
    _, rows, width, chan = images.shape
    nrow, ncol = lax.axis_size("row"), lax.axis_size("col")
    nz = nrow // 2
    scale = 1.0 / math.sqrt(MB * rows * nrow * width * ncol)
    dims = (rows, width, chan, nrow, ncol, scale)
    tall, wp = rows + 2 * REACH, width + 2 * PAD
    wide = width + 2 * SIDE
    half, strip = chan // 2, chan // 2 // ncol
    share = (TAPS - 1) // nz
    vm = pltpu.VMEM
    sems = 8 * 3 + 7 + 3 + 2 + 2 * (ncol - 1) + 2 * (nz - 1)
    anywhere = pl.BlockSpec(memory_space=pl.ANY)
    call = pl.pallas_call(
        functools.partial(body_kernel, dims),
        out_shape=(
            jax.ShapeDtypeStruct(images.shape, BF),
            jax.ShapeDtypeStruct(images.shape, BF),
            jax.ShapeDtypeStruct((TAPS, chan, chan), F32),
        ),
        in_specs=[anywhere] * 4,
        out_specs=(anywhere,) * 3,
        scratch_shapes=[
            vm((MB, tall, wide, chan), BF),
            vm((MB, rows + 2 * GREACH, wide, chan), BF),
            vm((SEG, TAPS, chan, chan), BF),
            vm((SEG, 1, chan), F32),
            vm((SEG, MB, tall // 2, 2, wp, 3 * chan), BF),
            vm((MB, tall // 2, 2, wp, chan), BF),
            vm((2, MB, tall // 2, 2, wp, 3 * chan), BF),
            vm((MB, tall // 2, 2, wp, chan), BF),
            vm((MB, rows + 4, wp, chan), BF),
            vm((SEG, 12 * chan, 2 * chan), BF),
            vm((SEG, 2 * chan, 12 * chan), BF),
            vm(images.shape, BF),
            vm(images.shape, BF),
            vm((TAPS, chan, chan), F32),
            vm((TAPS, chan, chan), F32),
            vm((TAPS, half, chan), BF),
            vm((TAPS, half, chan), BF),
            vm((TAPS, half, chan), F32),
            vm((TAPS, half, chan), BF),
            vm((ncol - 1, TAPS, strip, chan), BF),
            vm((nz, share + 1, strip, chan), BF),
            vm((nz, share + 1, strip, chan), BF),
            vm((TAPS, chan, chan), BF),
            pltpu.SemaphoreType.DMA((sems,)),
            pltpu.SemaphoreType.DMA((sems,)),
            pltpu.SemaphoreType.DMA((9,)),
        ],
        compiler_params=pltpu.CompilerParams(
            collective_id=0, has_side_effects=True, vmem_limit_bytes=56 * 2**20
        ),
    )
    outs, grads, kernels = call(
        images, cotangent, weights.reshape(TAPS, chan, chan), biases
    )
    return outs[None], grads[None], kernels.reshape(1, 3, 3, chan, chan)


def solution(mesh):
    placed = (
        P(None, "row", "col", None),
        P(None, "row", "col", None),
        P("segment", None, None, None, None),
        P("segment", None),
    )
    return jax.shard_map(
        body,
        mesh=mesh,
        in_specs=placed,
        out_specs=(
            P("segment", None, "row", "col", None),
            P("segment", None, "row", "col", None),
            P("segment", None, None, None, None),
        ),
        check_vma=False,
    )
```

time: 479 us -> 57.7 us (0.12)
  waiting for transfers between devices: 223 us -> 0 us
  starting transfers between devices: 200 us -> 0 us
  Pallas kernels: 0 us -> 52.7 us
  matrix products: 26.3 us -> 0 us
  between operations: 16.9 us -> 0.65 us
  other arithmetic: 6.37 us -> 0 us
    ppermute x68 -> x0, starting transfers between devices: 200 us -> none  [the longest x30 125 us: with_halo(): lax.ppermute(tail, axis, [(i, (i + 1) % count) for i in range(ends)])]
    psum x1 -> x0, waiting for transfers between devices: 186 us -> none  [body(): grad_total = lax.psum(grad_total, ('row', 'col'))]
    pallas_call x0 -> x1, Pallas kernels: none -> 52.7 us  [body(): call(images, cotangent, weights.reshape(TAPS, chan, chan), biases)]
    ppermute x68 -> x0, waiting for transfers between devices: 37.3 us -> none  [the longest x8 19.2 us: shifted(): return lax.ppermute(array, axis, pairs)]
    dot_general x135 -> x0, matrix products: 26.3 us -> none  [the longest x45 10.3 us: kernel_padded(): lax.dot_general(window, flat_grad, (((0,), (0,)), ((), ())), preferred_el...]
  transfers between devices with their start and end apart: 69 -> 0, of which waited for: 21 -> 0; matrix products, arithmetic and copies ran while one was open for 4% -> 0% of each run, Pallas kernels for 0% -> 0%
where the time goes in v1:
time: 57.7 us; the launch traced here: 57.5 us
  Pallas kernels  52.7 us (91%)
  local copies, waits for them, and re-layouts  4.22 us (7%)
  between operations  0.65 us (1%)
    pallas_call x1, Pallas kernels, body(): call(images, cotangent, weights.reshape(TAPS, chan, chan), biases)  52.7 us
    unnamed x5, local copies, waits for them, and re-layouts  4.22 us

profile of v1, /device:TPU:1, one launch (start us, length us, event | category | flops | bytes accessed | tf_op | source)
XLA Modules:
  0.0 57.5 jit_solution(8582477732688927818)
XLA Ops:
  0.6 52.7 %shard_map.67 = (bf16[2,8,64,128]{3,2,1,0:T(8,128)(2,1)}, bf16[2,8,64,128]{3,2,1,0:T(8,128)(2,1)}, f32[9,128,128]{2,1,0:T(8,128)}) custom-call(bf16[2,8,64,128]{3,2,1,0:T(8,128)(2,1)} %images.1, bf16[2,8,64,128]{3,2,1,0:T(8,128)(2,1)} %cot.1, bf16[9,128,128]{2,1,0:T(8,128)(2,1)} %bitcast.5, f32[1,128]{1,0:T(1,128)} %b.1), custom_call_target="tpu_custom_call" | custom-call | tf_op jit(solution)/shard_map/pallas_call | solution.py:499
  53.3 0.0 copy-start
  53.3 1.7 %copy.10 = bf16[1,2,8,64,128]{4,3,2,1,0:T(8,128)(2,1)} copy(bf16[1,2,8,64,128]{4,3,2,1,0:T(8,128)(2,1)} %bitcast.7) | data formatting | bytes 524288
  55.0 1.7 %copy.11 = bf16[1,2,8,64,128]{4,3,2,1,0:T(8,128)(2,1)} copy(bf16[1,2,8,64,128]{4,3,2,1,0:T(8,128)(2,1)} %bitcast.6) | data formatting | bytes 524288
  56.7 0.0 copy-done
  56.7 0.8 %copy.12 = f32[1,3,3,128,128]{4,3,2,1,0:T(8,128)} copy(f32[1,3,3,128,128]{4,3,2,1,0:T(8,128)S(1)} %bitcast.4) | data formatting | bytes 1179648
Async XLA Ops:
  53.3 3.4 %copy-start = (f32[9,128,128]{2,1,0:T(8,128)S(1)}, f32[9,128,128]{2,1,0:T(8,128)}, u32[]{:S(2)}) copy-start(f32[9,128,128]{2,1,0:T(8,128)} %get-tuple-element.8) | copy-start | bytes 1769476

commit v2 on v1

--- a/solution.py
+++ b/solution.py
@@ -14,16 +14,17 @@
 SEG, MB, TAPS = 4, 2, 9
 REACH = 6
 GREACH = 4
+WORDS = 5
 SIDE = 16
 PAD = 8
 DIRS = ((0, 1), (0, -1), (1, 0), (-1, 0), (1, 1), (1, -1), (-1, 1), (-1, -1))
 
 
 def body_kernel(
-    dims, images, cot, w, b, ox, og, ow,
-    xin, gin, wall, ball, aa, xs, gg, gs, gm, wf, wb, oxb, ogb, owb,
-    dw, s_core, r_core, d_half, s_col, r_col, s_row, r_row, full,
-    ss, rs, ls,
+    dims, images, cot, w, b, ox, og, full,
+    xin, gin, wall, ball, aa, xs, gg, gs, gm, wf, wb,
+    dw, s_core, r_core, d_half, r_main, r_extra,
+    ss, rs, ls, words,
 ):
     rows, width, chan, nrow, ncol, scale = dims
     nz = nrow // 2
@@ -35,15 +36,18 @@
     core, z = lax.rem(row, 2), lax.div(row, 2)
     sib = row + 1 - 2 * core
 
+    def both(step):
+        lax.fori_loop(0, MB, lambda m, carry: (step(m), carry)[1], 0)
+
     counter = [0]
 
     def fresh():
         counter[0] += 1
         return counter[0] - 1
 
-    def remote(src, dst, dev, i):
+    def remote(src, dst, dev, i, j=None):
         return pltpu.make_async_remote_copy(
-            src_ref=src, dst_ref=dst, send_sem=ss.at[i], recv_sem=rs.at[i],
+            src_ref=src, dst_ref=dst, send_sem=ss.at[i], recv_sem=rs.at[i if j is None else j],
             device_id=dev, device_id_type=MESH,
         )
 
@@ -72,16 +76,30 @@
 
     for k in range(1, SEG):
         greet(lax.rem(seg + k, SEG), row, col)
-    for k in range(1, ncol):
-        greet(seg, row, lax.rem(col + k, ncol))
-    for k in range(1, nz):
-        greet(seg, lax.rem(row + 2 * k, nrow), col)
-    met = SEG - 1 + ncol - 1 + nz - 1
+    beside_z = [lax.rem(row + 2, nrow), lax.rem(row + nrow - 2, nrow)]
+    beside_y = [lax.rem(col + 1, ncol), lax.rem(col + ncol - 1, ncol)]
+    for r in beside_z:
+        greet(seg, r, col)
+    for c in beside_y:
+        greet(seg, row, c)
+    met = SEG - 1 + 4
     for dr, dc in DIRS:
         if dr:
             pl.when(inside(dr, dc))(functools.partial(greet, seg, row + dr, col + dc))
             met = met + inside(dr, dc).astype(jnp.int32)
     pl.semaphore_wait(barrier, met)
+
+    def pass_word(n):
+        if n:
+            pl.semaphore_wait(words.at[n - 1], 2)
+        if n < nz // 2 - 1:
+            for r in beside_z:
+                pl.semaphore_signal(words.at[n], inc=1, device_id=(seg, r, col), device_id_type=MESH)
+        elif n < WORDS:
+            for c in beside_y:
+                pl.semaphore_signal(words.at[n], inc=1, device_id=(seg, row, c), device_id_type=MESH)
+
+    pass_word(0)
 
     def edges(source, target, reach):
         copies = []
@@ -121,15 +139,20 @@
     sib_rows = pl.ds(pl.multiple_of(half * (1 - core), half), half)
     up, down = (nxt, row, col), (prv, row, col)
     beside = (seg, sib, col)
-    i_up, i_down = fresh(), fresh()
-    w_up = remote(w.at[:, own_rows], wall.at[seg, :, own_rows], up, i_up)
-    w_down = remote(w.at[:, own_rows], wall.at[seg, :, own_rows], down, i_down)
-    got_prv = remote(w.at[:, own_rows], wall.at[prv, :, own_rows], up, i_up)
-    got_nxt = remote(w.at[:, own_rows], wall.at[nxt, :, own_rows], down, i_down)
+    i_ups, i_downs = (fresh(), fresh()), (fresh(), fresh())
+
+    def outward(part, dev, i):
+        return remote(w.at[:, part], wall.at[seg, :, part], dev, i)
 
     def onward(which, part, dev, i):
         return remote(wall.at[which, :, part], wall.at[which, :, part], dev, i)
 
+    w_out = [
+        outward(first_q, up, i_ups[0]), outward(second_q, down, i_downs[0]),
+        outward(second_q, up, i_ups[1]), outward(first_q, down, i_downs[1]),
+    ]
+    got_prv = [onward(prv, first_q, up, i_ups[0]), onward(prv, second_q, up, i_ups[1])]
+    got_nxt = [onward(nxt, second_q, down, i_downs[0]), onward(nxt, first_q, down, i_downs[1])]
     i_rup, i_rdown, i_s1, i_s2, i_s3 = fresh(), fresh(), fresh(), fresh(), fresh()
     relay_up, relay_down = onward(prv, first_q, up, i_rup), onward(nxt, second_q, down, i_rdown)
     got_rup, got_rdown = onward(far, first_q, up, i_rup), onward(far, second_q, down, i_rdown)
@@ -143,27 +166,34 @@
         b_out.append(remote(b, ball.at[seg], (lax.rem(seg + k, SEG), row, col), i))
         b_in.append(remote(b, ball.at[lax.rem(seg + SEG - k, SEG)], (lax.rem(seg + k, SEG), row, col), i))
 
-    w_up.start()
-    w_down.start()
     start_edges(x_edges[0])
+    for copy in w_out:
+        copy.start()
+    start_edges(x_edges[1])
     for copy in b_out:
         copy.start()
-    start_edges(x_edges[1])
     start_edges(g_edges)
 
-    got_prv.wait_recv()
-    relay_up.start()
-    share_prv.start()
-    got_nxt.wait_recv()
-    relay_down.start()
-    share_nxt.start()
+    def pass_near():
+        got_prv[0].wait_recv()
+        relay_up.start()
+        got_nxt[0].wait_recv()
+        relay_down.start()
+        got_prv[1].wait_recv()
+        share_prv.start()
+        got_nxt[1].wait_recv()
+        share_nxt.start()
 
     def pass_far():
         got_rup.wait_recv()
         got_rdown.wait_recv()
         share_far.start()
 
-    pl.when(seg == 2)(pass_far)
+    def need(k):
+        pl.when(seg == k)(mine_w.wait)
+        pl.when(nxt == k)(got_s2.wait_recv)
+        pl.when(far == k)(got_s3.wait_recv)
+        pl.when(prv == k)(got_s1.wait_recv)
 
     def in_image(first, step, count):
         shape = (count, wp, chan)
@@ -186,10 +216,9 @@
         for t, part in enumerate(trio(jnp.maximum(v, 0.0))):
             aa[0, m, :, :, :, pl.ds(t * chan, chan)] = part.reshape(tall // 2, 2, wp, chan)
 
-    for m in range(MB):
+    def wait_in(m):
         mine[m].wait()
         wait_edges(x_edges[m])
-        take_in(m)
 
     def build(k):
         zero = jnp.zeros((3 * chan, chan), BF)
@@ -228,50 +257,50 @@
         lo, up_to = REACH // 2, hi // 2
         return ref[m, lo:up_to].reshape(rows, wp, chan).astype(F32)
 
-    x_done = pltpu.make_async_copy(oxb, ox, ls.at[5])
-    g_done = pltpu.make_async_copy(ogb, og, ls.at[6])
-
     def emit_x():
-        for m in range(MB):
-            oxb[m] = block_of(xs, m)[:, PAD : PAD + width].astype(BF)
-        x_done.start()
+        def one(m):
+            ox[m] = block_of(xs, m)[:, PAD : PAD + width].astype(BF)
+
+        both(one)
 
     def emit_g():
-        for m in range(MB):
-            ogb[m] = block_of(gs, m)[:, PAD : PAD + width].astype(BF)
-        g_done.start()
-
-    mine_w.wait()
+        def one(m):
+            og[m] = block_of(gs, m)[:, PAD : PAD + width].astype(BF)
+
+        both(one)
+
+    wait_in(0)
+    pass_near()
+    pl.when(seg == 2)(pass_far)
+    need(0)
     mine_b.wait()
     for copy in b_in:
         copy.wait_recv()
-    got_s1.wait_recv()
-    got_s2.wait_recv()
-    pl.when(seg == 2)(got_s3.wait_recv)
     build(0)
-    forward(0, 0)
-    pl.when(seg != 2)(pass_far)
-    forward(0, 1)
+    wait_in(1)
+    both(take_in)
+    both(lambda m: forward(0, m))
+    pass_word(1)
+    pl.when(seg == 3)(pass_far)
     pl.when(seg == 0)(emit_x)
-    pl.when(seg != 2)(got_s3.wait_recv)
-    for s in range(1, SEG - 1):
-        build(s)
-        for m in range(MB):
-            forward(s, m)
-        pl.when(seg == s)(emit_x)
-    build(SEG - 1)
-
-    def last():
-        for m in range(MB):
-            forward(SEG - 1, m)
-        emit_x()
-
-    pl.when(seg == SEG - 1)(last)
+    need(1)
+    build(1)
+    both(lambda m: forward(1, m))
+    pass_word(2)
+    pl.when(seg < 2)(pass_far)
+    pl.when(seg == 1)(emit_x)
+    need(2)
+    build(2)
+    both(lambda m: forward(2, m))
+    pass_word(3)
+    pl.when(seg == 2)(emit_x)
+    need(3)
+    build(3)
 
     mine_g.wait()
     wait_edges(g_edges)
     edge = REACH - GREACH
-    for m in range(MB):
+    def take_in_grad(m):
         v = gin[m].astype(F32)[:, PAD : PAD + wp]
         v = jnp.where(in_image(edge, 1, tall - 2 * edge), v, 0.0)
         lo, n = edge // 2, tall // 2 - edge
@@ -282,16 +311,19 @@
         gm[m, 0:2] = nothing
         gm[m, rows + 2 : rows + 4] = nothing
 
+    both(take_in_grad)
+
     def keep():
         c = lax.broadcasted_iota(jnp.int32, (rows, wp, chan), 1)
-        for m in range(MB):
+        def one(m):
             v = jnp.where((c >= PAD) & (c < PAD + width), block_of(gs, m), 0.0)
             gm[m, 2 : rows + 2] = v.astype(BF)
 
-    def backward(k, m):
-        start, count = REACH - k, rows + 2 * k
+        both(one)
+
+    def backward(k, m, slot, start, count, more):
         y = lax.dot_general(
-            windows(gg.at[k % 2, m], start, count), wb[k], (((1,), (1,)), ((), ())),
+            windows(gg.at[slot, m], start, count), wb[k], (((1,), (1,)), ((), ())),
             preferred_element_type=F32,
         )
         for h in range(2):
@@ -301,20 +333,26 @@
             g = gs[m, i : i + n, par].astype(F32)
             g = (g + jnp.where(on, y[:, h * chan : (h + 1) * chan].reshape(n, wp, chan), 0.0)).astype(BF)
             gs[m, i : i + n, par] = g
-            if k:
+            if more:
                 for t, part in enumerate(trio(g.astype(F32))):
-                    gg[(k - 1) % 2, m, i : i + n, par, :, pl.ds(t * chan, chan)] = part
+                    gg[1 - slot, m, i : i + n, par, :, pl.ds(t * chan, chan)] = part
 
     for k in range(SEG - 1, 0, -1):
-        pl.when(seg == k)(keep)
 
         def stage(k=k):
-            for m in range(MB):
-                backward(k, m)
-
-        pl.when(seg <= k)(stage)
-        pl.when(seg == k)(emit_g)
-    pl.when(seg == 0)(keep)
+            both(lambda m: backward(k, m, k % 2, REACH - k, rows + 2 * k, True))
+
+        pl.when(seg < k)(stage)
+        if k == SEG - 1:
+            pass_word(4)
+    keep()
+
+    def own_grad(m):
+        backward(seg, m, lax.rem(seg, 2), REACH, rows, False)
+
+    def last_x():
+        both(lambda m: forward(SEG - 1, m))
+        emit_x()
 
     total = None
     for m in range(MB):
@@ -338,108 +376,162 @@
         for _, copy in pairs:
             copy.wait_recv()
 
-    late = []
+    pass_word(5)
     s_core[...] = dw[:, sib_rows].astype(BF)
     i = fresh()
-    core_sum = exchange([(remote(s_core, r_core, beside, i),) * 2])
-    late += core_sum
-    pl.when(seg == 0)(lambda: backward(0, 0))
-    arrived(core_sum)
-    d_half[...] = dw[:, own_rows] + r_core[...].astype(F32)
-    s_col[...] = d_half[...].astype(BF)
-    my_strip = pl.ds(pl.multiple_of(strip * col, strip), strip)
-    col_sum = []
-    for k in range(1, ncol):
-        to = lax.rem(col + k, ncol)
-        copy = remote(
-            s_col.at[:, pl.ds(pl.multiple_of(strip * to, strip), strip)], r_col.at[k - 1],
-            (seg, row, to), fresh(),
+    core_sum = remote(s_core, r_core, beside, i)
+    core_sum.start()
+    own_grad(0)
+    core_sum.wait_recv()
+    d_half[...] = (dw[:, own_rows] + r_core[...].astype(F32)).astype(BF)
+
+    share = (TAPS - 1) // nz
+    here = col * nz + z
+    steps = [(ky, kz) for ky in range(ncol) for kz in range(nz) if ky or kz]
+
+    def strip_of(c):
+        return pl.ds(pl.multiple_of(strip * c, strip), strip)
+
+    def place_of(c):
+        return pl.ds(pl.multiple_of(half * core + strip * c, strip), strip)
+
+    def taps_of(r):
+        return pl.ds(r * share, share)
+
+    def owner(c):
+        return c * nz // ncol
+
+    def peer(ky, kz, sign):
+        return lax.rem(col + ncol + sign * ky, ncol), lax.rem(z + nz + sign * kz, nz)
+
+    sums = []
+    for ky, kz in steps:
+        (c, r), (oc, orow) = peer(ky, kz, 1), peer(ky, kz, -1)
+        i = fresh()
+        src = d_half.at[taps_of(r), strip_of(c)]
+        dev = (seg, 2 * r + core, c)
+        sums.append((remote(src, r_main.at[here], dev, i), remote(src, r_main.at[oc * nz + orow], dev, i)))
+    base_send, base_recv = counter[0], counter[0] + ncol
+    counter[0] += ncol + nz * ncol
+    extra_out, extra_in = [], []
+    last_tap = pl.ds(TAPS - 1, 1)
+    for ky in range(ncol):
+        c = lax.rem(col + ky, ncol)
+        r = owner(c)
+        at = ky * nz + lax.rem(r - z + nz, nz)
+        extra_out.append((
+            remote(
+                d_half.at[last_tap, strip_of(c)], r_extra.at[here],
+                (seg, 2 * r + core, c), base_send + ky, base_recv + at,
+            ),
+            at > 0,
+        ))
+    for ky, kz in steps:
+        oc, orow = peer(ky, kz, -1)
+        extra_in.append(remote(
+            d_half.at[last_tap, strip_of(col)], r_extra.at[oc * nz + orow],
+            beside, base_send, base_recv + ky * nz + kz,
+        ))
+    for copy, on in extra_out:
+        pl.when(on)(copy.start)
+    for copy, _ in sums:
+        copy.start()
+    r_main[here] = d_half[taps_of(z), strip_of(col)]
+    own = z == owner(col)
+
+    def put_extra():
+        r_extra[here] = d_half[last_tap, strip_of(col)]
+
+    pl.when(own)(put_extra)
+    own_grad(1)
+    emit_g()
+    pl.when(seg == SEG - 1)(last_x)
+
+    def total_of(ref):
+        done = ref[0].astype(F32)
+        for k in range(1, ncol * nz):
+            done = done + ref[k].astype(F32)
+        return (done * scale).astype(BF)
+
+    spread, spread_extra = [], []
+    for ky, kz in steps:
+        (c, r), (oc, orow) = peer(ky, kz, 1), peer(ky, kz, -1)
+        i = fresh()
+        src = full.at[taps_of(z), place_of(col)]
+        dev = (seg, 2 * r + core, c)
+        spread.append((remote(src, src, dev, i), remote(src, full.at[taps_of(orow), place_of(oc)], dev, i)))
+    base_send = counter[0]
+    base_recv = counter[0] + len(steps)
+    counter[0] += len(steps) + ncol
+    for n, (ky, kz) in enumerate(steps):
+        c, r = peer(ky, kz, 1)
+        src = full.at[last_tap, place_of(col)]
+        spread_extra.append(
+            remote(src, src, (seg, 2 * r + core, c), base_send + n, base_recv + col)
         )
-        col_sum.append((copy, copy))
-    exchange(col_sum)
-    late += col_sum
-
-    def final_g():
-        backward(0, 1)
-        emit_g()
-
-    pl.when(seg == 0)(final_g)
-    arrived(col_sum)
-    part = d_half[:, my_strip]
-    for k in range(1, ncol):
-        part = part + r_col[k - 1].astype(F32)
-    part = part.astype(BF)
-    share = (TAPS - 1) // nz
-    for to in range(nz):
-        s_row[to, 0:share] = part[to * share : (to + 1) * share]
-        s_row[to, share : share + 1] = part[TAPS - 1 :]
-    r_row[z] = s_row[z]
-    row_sum = []
-    for k in range(1, nz):
-        to, of = lax.rem(z + k, nz), lax.rem(z + nz - k, nz)
-        dev, i = (seg, 2 * to + core, col), fresh()
-        row_sum.append((
-            remote(s_row.at[to], r_row.at[z], dev, i), remote(s_row.at[to], r_row.at[of], dev, i)
+    got_extra = []
+    for c in range(ncol):
+        src = full.at[last_tap, place_of(c)]
+        got_extra.append((
+            remote(src, src, beside, base_send, base_recv + c),
+            (col != c) | (z != owner(c)),
         ))
-    exchange(row_sum)
-    late += row_sum
-    arrived(row_sum)
-    done = r_row[0].astype(F32)
-    for k in range(1, nz):
-        done = done + r_row[k].astype(F32)
-    done = (done * scale).astype(BF)
-    place = pl.ds(pl.multiple_of(half * core + strip * col, strip), strip)
-    full[pl.ds(z * share, share), place] = done[:share]
-    full[TAPS - 1 :, place] = done[share:]
-
-    def spread(part_of):
-        return full.at[pl.ds(part_of * share, share), place]
-
-    row_all = []
-    for k in range(1, nz):
-        to, of = lax.rem(z + k, nz), lax.rem(z + nz - k, nz)
-        dev, i = (seg, 2 * to + core, col), fresh()
-        row_all.append((remote(spread(z), spread(z), dev, i), remote(spread(z), spread(of), dev, i)))
-    exchange(row_all)
-    late += row_all
-    arrived(row_all)
-
-    def column(c):
-        return full.at[:, pl.ds(pl.multiple_of(half * core + strip * c, strip), strip)]
-
-    col_all = []
-    for k in range(1, ncol):
-        to, of = lax.rem(col + k, ncol), lax.rem(col + ncol - k, ncol)
-        dev, i = (seg, row, to), fresh()
-        col_all.append((remote(column(col), column(col), dev, i), remote(column(col), column(of), dev, i)))
-    exchange(col_all)
-    late += col_all
-    arrived(col_all)
-    i = fresh()
-    core_all = exchange([(
-        remote(full.at[:, own_rows], full.at[:, own_rows], beside, i),
-        remote(full.at[:, own_rows], full.at[:, sib_rows], beside, i),
-    )])
-    late += core_all
-    owb[:, own_rows] = full[:, own_rows].astype(F32)
-    out_own = pltpu.make_async_copy(owb.at[:, own_rows], ow.at[:, own_rows], ls.at[7])
-    out_own.start()
+
+    for _, copy in sums:
+        copy.wait_recv()
+    full[taps_of(z), place_of(col)] = total_of(r_main)
+    for copy, _ in spread:
+        copy.start()
+
+    def finish_extra():
+        for copy in extra_in:
+            copy.wait_recv()
+        full[last_tap, place_of(col)] = total_of(r_extra)
+        for copy in spread_extra:
+            copy.start()
+
+    pl.when(own)(finish_extra)
 
     for copies in (*x_edges, g_edges):
         for copy, to, _ in copies:
             pl.when(to)(copy.wait_send)
-    for copy in (w_up, w_down, relay_up, relay_down, share_prv, share_nxt, share_far, *b_out):
+    for copy in (*w_out, relay_up, relay_down, share_prv, share_nxt, share_far, *b_out):
         copy.wait_send()
-    arrived(core_all)
-    owb[:, sib_rows] = full[:, sib_rows].astype(F32)
-    out_sib = pltpu.make_async_copy(owb.at[:, sib_rows], ow.at[:, sib_rows], ls.at[8])
-    out_sib.start()
-    for copy, _ in late:
+    for copy, _ in sums:
         copy.wait_send()
-    x_done.wait()
-    g_done.wait()
-    out_own.wait()
-    out_sib.wait()
+    for copy, on in extra_out:
+        pl.when(on)(copy.wait_send)
+    core_sum.wait_send()
+
+    for _, copy in spread:
+        copy.wait_recv()
+    for copy, on in got_extra:
+        pl.when(on)(copy.wait_recv)
+    i = fresh()
+    core_all = remote(full.at[:, own_rows], full.at[:, own_rows], beside, i)
+    core_got = remote(full.at[:, own_rows], full.at[:, sib_rows], beside, i)
+    core_all.start()
+    for copy, _ in spread:
+        copy.wait_send()
+
+    def extra_left():
+        for copy in spread_extra:
+            copy.wait_send()
+
+    pl.when(own)(extra_left)
+    core_got.wait_recv()
+    core_all.wait_send()
+
+
+def write_kernel(x, g, k, ox, og, ow, buf, sems):
+    copies = [pltpu.make_async_copy(x, ox, sems.at[0]), pltpu.make_async_copy(g, og, sems.at[1])]
+    for copy in copies:
+        copy.start()
+    buf[...] = k[...].astype(F32)
+    copies.append(pltpu.make_async_copy(buf, ow, sems.at[2]))
+    copies[-1].start()
+    for copy in copies:
+        copy.wait()
 
 
 def body(images, cotangent, weights, biases):
@@ -453,17 +545,15 @@
     half, strip = chan // 2, chan // 2 // ncol
     share = (TAPS - 1) // nz
     vm = pltpu.VMEM
-    sems = 8 * 3 + 7 + 3 + 2 + 2 * (ncol - 1) + 2 * (nz - 1)
+    chips = ncol * nz
+    sems = 8 * 3 + 9 + 3 + 2 + 4 * chips + 2 * ncol
     anywhere = pl.BlockSpec(memory_space=pl.ANY)
+    inside = pl.BlockSpec(memory_space=pltpu.VMEM)
     call = pl.pallas_call(
         functools.partial(body_kernel, dims),
-        out_shape=(
-            jax.ShapeDtypeStruct(images.shape, BF),
-            jax.ShapeDtypeStruct(images.shape, BF),
-            jax.ShapeDtypeStruct((TAPS, chan, chan), F32),
-        ),
+        out_shape=(vm(images.shape, BF), vm(images.shape, BF), vm((TAPS, chan, chan), BF)),
         in_specs=[anywhere] * 4,
-        out_specs=(anywhere,) * 3,
+        out_specs=(inside,) * 3,
         scratch_shapes=[
             vm((MB, tall, wide, chan), BF),
             vm((MB, rows + 2 * GREACH, wide, chan), BF),
@@ -476,29 +566,34 @@
             vm((MB, rows + 4, wp, chan), BF),
             vm((SEG, 12 * chan, 2 * chan), BF),
             vm((SEG, 2 * chan, 12 * chan), BF),
-            vm(images.shape, BF),
-            vm(images.shape, BF),
-            vm((TAPS, chan, chan), F32),
             vm((TAPS, chan, chan), F32),
             vm((TAPS, half, chan), BF),
             vm((TAPS, half, chan), BF),
-            vm((TAPS, half, chan), F32),
             vm((TAPS, half, chan), BF),
-            vm((ncol - 1, TAPS, strip, chan), BF),
-            vm((nz, share + 1, strip, chan), BF),
-            vm((nz, share + 1, strip, chan), BF),
-            vm((TAPS, chan, chan), BF),
+            vm((chips, share, strip, chan), BF),
+            vm((chips, 1, strip, chan), BF),
             pltpu.SemaphoreType.DMA((sems,)),
             pltpu.SemaphoreType.DMA((sems,)),
-            pltpu.SemaphoreType.DMA((9,)),
+            pltpu.SemaphoreType.DMA((5,)),
+            pltpu.SemaphoreType.REGULAR((WORDS,)),
         ],
         compiler_params=pltpu.CompilerParams(
             collective_id=0, has_side_effects=True, vmem_limit_bytes=56 * 2**20
         ),
     )
-    outs, grads, kernels = call(
-        images, cotangent, weights.reshape(TAPS, chan, chan), biases
-    )
+    results = call(images, cotangent, weights.reshape(TAPS, chan, chan), biases)
+    outs, grads, kernels = pl.pallas_call(
+        write_kernel,
+        out_shape=(
+            jax.ShapeDtypeStruct(images.shape, BF),
+            jax.ShapeDtypeStruct(images.shape, BF),
+            jax.ShapeDtypeStruct((TAPS, chan, chan), F32),
+        ),
+        in_specs=[inside] * 3,
+        out_specs=(anywhere,) * 3,
+        scratch_shapes=[vm((TAPS, chan, chan), F32), pltpu.SemaphoreType.DMA((3,))],
+        compiler_params=pltpu.CompilerParams(vmem_limit_bytes=4 * 2**20),
+    )(*results)
     return outs[None], grads[None], kernels.reshape(1, 3, 3, chan, chan)
 
 

time: 57.7 us -> 52.4 us (0.908)
  local copies, waits for them, and re-layouts: 4.22 us -> 0 us
  Pallas kernels: 52.7 us -> 51.7 us
    unnamed x5 -> x0, local copies, waits for them, and re-layouts: 4.22 us -> none
    pallas_call x1 -> x2, Pallas kernels: 52.7 us -> 51.7 us  [the longest x1 50.7 us: body(): results = call(images, cotangent, weights.reshape(TAPS, chan, chan), biases)]
where the time goes in v2:
time: 52.4 us
  Pallas kernels  51.7 us (99%)
  between operations  0.64 us (1%)
    pallas_call x1, Pallas kernels, body(): results = call(images, cotangent, weights.reshape(TAPS, chan, chan), biases)  50.7 us

profile of v2, /device:TPU:1, one launch (start us, length us, event | category | flops | bytes accessed | tf_op | source)
XLA Modules:
  0.0 52.4 jit_solution(8873250492397590231)
XLA Ops:
  0.6 50.7 %shard_map.67 = (bf16[2,8,64,128]{3,2,1,0:T(8,128)(2,1)S(1)}, bf16[2,8,64,128]{3,2,1,0:T(8,128)(2,1)S(1)}, bf16[9,128,128]{2,1,0:T(8,128)(2,1)S(1)}) custom-call(bf16[2,8,64,128]{3,2,1,0:T(8,128)(2,1)} %images.1, bf16[2,8,64,128]{3,2,1,0:T(8,128)(2,1)} %cot.1, bf16[9,128,128]{2,1,0:T(8,128)(2,1)} %bitcast.4, f32[1,128]{1,0:T(1,128)} %b.1), custom_call_target="tpu_custom_call" | custom-call | tf_op jit(solution)/shard_map/pallas_call | solution.py:584
  51.3 1.0 %shard_map.68 = (bf16[2,8,64,128]{3,2,1,0:T(8,128)(2,1)}, bf16[2,8,64,128]{3,2,1,0:T(8,128)(2,1)}, f32[9,128,128]{2,1,0:T(8,128)}) custom-call(bf16[2,8,64,128]{3,2,1,0:T(8,128)(2,1)S(1)} %get-tuple-element.9.x, bf16[2,8,64,128]{3,2,1,0:T(8,128)(2,1)S(1)} %get-tuple-element.10.g, bf16[9,128,128]{2,1,0:T(8,128)(2,1)S(1)} %get-tuple-element.11.k), custom_call_target="tpu_custom_call" | custom-call | tf_op jit(solution)/shard_map/pallas_call | solution.py:585

commit v3 on v2

--- a/solution.py
+++ b/solution.py
@@ -20,10 +20,14 @@
 DIRS = ((0, 1), (0, -1), (1, 0), (-1, 0), (1, 1), (1, -1), (-1, 1), (-1, -1))
 
 
+def wrap(v, n):
+    return jnp.where(v >= n, v - n, v)
+
+
 def body_kernel(
     dims, images, cot, w, b, ox, og, full,
     xin, gin, wall, ball, aa, xs, gg, gs, gm, wf, wb,
-    dw, s_core, r_core, d_half, r_main, r_extra,
+    dw, s_core, r_core, d_half, r_main, r_tap_col, s_tap, r_tap_row,
     ss, rs, ls, words,
 ):
     rows, width, chan, nrow, ncol, scale = dims
@@ -270,29 +274,32 @@
         both(one)
 
     wait_in(0)
+    take_in(0)
     pass_near()
+    pass_word(1)
     pl.when(seg == 2)(pass_far)
     need(0)
     mine_b.wait()
     for copy in b_in:
         copy.wait_recv()
     build(0)
+    forward(0, 0)
     wait_in(1)
-    both(take_in)
-    both(lambda m: forward(0, m))
-    pass_word(1)
+    take_in(1)
+    forward(0, 1)
+    pass_word(2)
     pl.when(seg == 3)(pass_far)
     pl.when(seg == 0)(emit_x)
     need(1)
     build(1)
     both(lambda m: forward(1, m))
-    pass_word(2)
+    pass_word(3)
     pl.when(seg < 2)(pass_far)
     pl.when(seg == 1)(emit_x)
     need(2)
     build(2)
     both(lambda m: forward(2, m))
-    pass_word(3)
+    pass_word(4)
     pl.when(seg == 2)(emit_x)
     need(3)
     build(3)
@@ -344,7 +351,7 @@
 
         pl.when(seg < k)(stage)
         if k == SEG - 1:
-            pass_word(4)
+            pass_word(5)
     keep()
 
     def own_grad(m):
@@ -376,7 +383,6 @@
         for _, copy in pairs:
             copy.wait_recv()
 
-    pass_word(5)
     s_core[...] = dw[:, sib_rows].astype(BF)
     i = fresh()
     core_sum = remote(s_core, r_core, beside, i)
@@ -386,139 +392,108 @@
     d_half[...] = (dw[:, own_rows] + r_core[...].astype(F32)).astype(BF)
 
     share = (TAPS - 1) // nz
-    here = col * nz + z
+    main = TAPS - 1
+    last_tap = pl.ds(main, 1)
+    cols = [wrap(col + k, ncol) for k in range(ncol)]
+    zs = [wrap(z + k, nz) for k in range(nz)]
+    strips = [pl.ds(pl.multiple_of(strip * c, strip), strip) for c in cols]
+    places = [pl.ds(pl.multiple_of(half * core + strip * c, strip), strip) for c in cols]
+    taps = [pl.ds(r * share, share) for r in zs]
+    slots = [[c * nz + r for r in zs] for c in cols]
     steps = [(ky, kz) for ky in range(ncol) for kz in range(nz) if ky or kz]
-
-    def strip_of(c):
-        return pl.ds(pl.multiple_of(strip * c, strip), strip)
-
-    def place_of(c):
-        return pl.ds(pl.multiple_of(half * core + strip * c, strip), strip)
-
-    def taps_of(r):
-        return pl.ds(r * share, share)
-
-    def owner(c):
-        return c * nz // ncol
-
-    def peer(ky, kz, sign):
-        return lax.rem(col + ncol + sign * ky, ncol), lax.rem(z + nz + sign * kz, nz)
+    steps.sort(key=lambda s: -min(s[0], ncol - s[0]) - min(s[1], nz - s[1]))
+
+    def device(ky, kz):
+        return seg, 2 * zs[kz] + core, cols[ky]
+
+    tap_col = [
+        remote(d_half.at[last_tap, strips[k]], r_tap_col.at[k - 1], device(k, 0), fresh())
+        for k in range(1, ncol)
+    ]
+    for copy in tap_col:
+        copy.start()
 
     sums = []
     for ky, kz in steps:
-        (c, r), (oc, orow) = peer(ky, kz, 1), peer(ky, kz, -1)
         i = fresh()
-        src = d_half.at[taps_of(r), strip_of(c)]
-        dev = (seg, 2 * r + core, c)
-        sums.append((remote(src, r_main.at[here], dev, i), remote(src, r_main.at[oc * nz + orow], dev, i)))
-    base_send, base_recv = counter[0], counter[0] + ncol
-    counter[0] += ncol + nz * ncol
-    extra_out, extra_in = [], []
-    last_tap = pl.ds(TAPS - 1, 1)
-    for ky in range(ncol):
-        c = lax.rem(col + ky, ncol)
-        r = owner(c)
-        at = ky * nz + lax.rem(r - z + nz, nz)
-        extra_out.append((
-            remote(
-                d_half.at[last_tap, strip_of(c)], r_extra.at[here],
-                (seg, 2 * r + core, c), base_send + ky, base_recv + at,
-            ),
-            at > 0,
+        src = d_half.at[taps[kz], strips[ky]]
+        sums.append((
+            remote(src, r_main.at[slots[0][0]], device(ky, kz), i),
+            remote(src, r_main.at[slots[-ky % ncol][-kz % nz]], device(ky, kz), i),
         ))
-    for ky, kz in steps:
-        oc, orow = peer(ky, kz, -1)
-        extra_in.append(remote(
-            d_half.at[last_tap, strip_of(col)], r_extra.at[oc * nz + orow],
-            beside, base_send, base_recv + ky * nz + kz,
-        ))
-    for copy, on in extra_out:
-        pl.when(on)(copy.start)
     for copy, _ in sums:
         copy.start()
-    r_main[here] = d_half[taps_of(z), strip_of(col)]
-    own = z == owner(col)
-
-    def put_extra():
-        r_extra[here] = d_half[last_tap, strip_of(col)]
-
-    pl.when(own)(put_extra)
+    r_main[slots[0][0]] = d_half[taps[0], strips[0]]
     own_grad(1)
     emit_g()
     pl.when(seg == SEG - 1)(last_x)
 
-    def total_of(ref):
+    def total_of(ref, count):
         done = ref[0].astype(F32)
-        for k in range(1, ncol * nz):
+        for k in range(1, count):
             done = done + ref[k].astype(F32)
-        return (done * scale).astype(BF)
-
-    spread, spread_extra = [], []
+        return done
+
+    for copy in tap_col:
+        copy.wait_recv()
+    tap = d_half[last_tap, strips[0]].astype(F32) + total_of(r_tap_col, ncol - 1)
+    s_tap[...] = tap.astype(BF)
+    r_tap_row[z] = tap.astype(BF)
+    tap_row = []
+    for k in range(1, nz):
+        i = fresh()
+        tap_row.append((
+            remote(s_tap, r_tap_row.at[z], device(0, k), i),
+            remote(s_tap, r_tap_row.at[zs[nz - k]], device(0, k), i),
+        ))
+    for copy, _ in tap_row:
+        copy.start()
+
+    spread = []
     for ky, kz in steps:
-        (c, r), (oc, orow) = peer(ky, kz, 1), peer(ky, kz, -1)
         i = fresh()
-        src = full.at[taps_of(z), place_of(col)]
-        dev = (seg, 2 * r + core, c)
-        spread.append((remote(src, src, dev, i), remote(src, full.at[taps_of(orow), place_of(oc)], dev, i)))
-    base_send = counter[0]
-    base_recv = counter[0] + len(steps)
-    counter[0] += len(steps) + ncol
-    for n, (ky, kz) in enumerate(steps):
-        c, r = peer(ky, kz, 1)
-        src = full.at[last_tap, place_of(col)]
-        spread_extra.append(
-            remote(src, src, (seg, 2 * r + core, c), base_send + n, base_recv + col)
-        )
-    got_extra = []
-    for c in range(ncol):
-        src = full.at[last_tap, place_of(c)]
-        got_extra.append((
-            remote(src, src, beside, base_send, base_recv + c),
-            (col != c) | (z != owner(c)),
+        src = full.at[taps[0], places[0]]
+        spread.append((
+            remote(src, src, device(ky, kz), i),
+            remote(src, full.at[taps[-kz % nz], places[-ky % ncol]], device(ky, kz), i),
         ))
-
     for _, copy in sums:
         copy.wait_recv()
-    full[taps_of(z), place_of(col)] = total_of(r_main)
+    full[taps[0], places[0]] = (total_of(r_main, ncol * nz) * scale).astype(BF)
     for copy, _ in spread:
         copy.start()
-
-    def finish_extra():
-        for copy in extra_in:
-            copy.wait_recv()
-        full[last_tap, place_of(col)] = total_of(r_extra)
-        for copy in spread_extra:
-            copy.start()
-
-    pl.when(own)(finish_extra)
+    for _, copy in tap_row:
+        copy.wait_recv()
+    full[last_tap, places[0]] = (total_of(r_tap_row, nz) * scale).astype(BF)
+    tap_all = []
+    for k in range(1, ncol):
+        i = fresh()
+        src = full.at[last_tap, places[0]]
+        tap_all.append((
+            remote(src, src, device(k, 0), i),
+            remote(src, full.at[last_tap, places[ncol - k]], device(k, 0), i),
+        ))
+    for copy, _ in tap_all:
+        copy.start()
 
     for copies in (*x_edges, g_edges):
         for copy, to, _ in copies:
             pl.when(to)(copy.wait_send)
     for copy in (*w_out, relay_up, relay_down, share_prv, share_nxt, share_far, *b_out):
         copy.wait_send()
-    for copy, _ in sums:
+    for copy, _ in (*sums, *tap_row):
         copy.wait_send()
-    for copy, on in extra_out:
-        pl.when(on)(copy.wait_send)
-    core_sum.wait_send()
-
-    for _, copy in spread:
+    for copy in (core_sum, *tap_col):
+        copy.wait_send()
+
+    for _, copy in (*spread, *tap_all):
         copy.wait_recv()
-    for copy, on in got_extra:
-        pl.when(on)(copy.wait_recv)
     i = fresh()
     core_all = remote(full.at[:, own_rows], full.at[:, own_rows], beside, i)
     core_got = remote(full.at[:, own_rows], full.at[:, sib_rows], beside, i)
     core_all.start()
-    for copy, _ in spread:
+    for copy, _ in (*spread, *tap_all):
         copy.wait_send()
-
-    def extra_left():
-        for copy in spread_extra:
-            copy.wait_send()
-
-    pl.when(own)(extra_left)
     core_got.wait_recv()
     core_all.wait_send()
 
@@ -546,7 +521,7 @@
     share = (TAPS - 1) // nz
     vm = pltpu.VMEM
     chips = ncol * nz
-    sems = 8 * 3 + 9 + 3 + 2 + 4 * chips + 2 * ncol
+    sems = 8 * 3 + 9 + 3 + 2 + 2 * (chips - 1) + 2 * (ncol - 1) + nz - 1
     anywhere = pl.BlockSpec(memory_space=pl.ANY)
     inside = pl.BlockSpec(memory_space=pltpu.VMEM)
     call = pl.pallas_call(
@@ -571,7 +546,9 @@
             vm((TAPS, half, chan), BF),
             vm((TAPS, half, chan), BF),
             vm((chips, share, strip, chan), BF),
-            vm((chips, 1, strip, chan), BF),
+            vm((ncol - 1, 1, strip, chan), BF),
+            vm((1, strip, chan), BF),
+            vm((nz, 1, strip, chan), BF),
             pltpu.SemaphoreType.DMA((sems,)),
             pltpu.SemaphoreType.DMA((sems,)),
             pltpu.SemaphoreType.DMA((5,)),

time: 52.4 us -> 48.1 us (0.918)
  Pallas kernels: 51.7 us -> 47.4 us
    pallas_call x1, Pallas kernels: 50.7 us -> 46.4 us  [body(): results = call(images, cotangent, weights.reshape(TAPS, chan, chan), biases)]
where the time goes in v3:
time: 48.1 us; the launch traced here: 48 us
  Pallas kernels  47.4 us (99%)
  between operations  0.64 us (1%)
    pallas_call x1, Pallas kernels, body(): results = call(images, cotangent, weights.reshape(TAPS, chan, chan), biases)  46.4 us
    pallas_call x1, Pallas kernels, body(): pl.pallas_call(write_kernel, out_shape=(jax.ShapeDtypeStruct(images.shape...  1.02 us

profile of v3, /device:TPU:1, one launch (start us, length us, event | category | flops | bytes accessed | tf_op | source)
XLA Modules:
  0.0 48.0 jit_solution(3235738041983684294)
XLA Ops:
  0.6 46.4 %shard_map.67 = (bf16[2,8,64,128]{3,2,1,0:T(8,128)(2,1)S(1)}, bf16[2,8,64,128]{3,2,1,0:T(8,128)(2,1)S(1)}, bf16[9,128,128]{2,1,0:T(8,128)(2,1)S(1)}) custom-call(bf16[2,8,64,128]{3,2,1,0:T(8,128)(2,1)} %images.1, bf16[2,8,64,128]{3,2,1,0:T(8,128)(2,1)} %cot.1, bf16[9,128,128]{2,1,0:T(8,128)(2,1)} %bitcast.4, f32[1,128]{1,0:T(1,128)} %b.1), custom_call_target="tpu_custom_call" | custom-call | tf_op jit(solution)/shard_map/pallas_call | solution.py:561
  47.0 1.0 %shard_map.68 = (bf16[2,8,64,128]{3,2,1,0:T(8,128)(2,1)}, bf16[2,8,64,128]{3,2,1,0:T(8,128)(2,1)}, f32[9,128,128]{2,1,0:T(8,128)}) custom-call(bf16[2,8,64,128]{3,2,1,0:T(8,128)(2,1)S(1)} %get-tuple-element.9.x, bf16[2,8,64,128]{3,2,1,0:T(8,128)(2,1)S(1)} %get-tuple-element.10.g, bf16[9,128,128]{2,1,0:T(8,128)(2,1)S(1)} %get-tuple-element.11.k), custom_call_target="tpu_custom_call" | custom-call | tf_op jit(solution)/shard_map/pallas_call | solution.py:562

commit v4 on v3

--- a/solution.py
+++ b/solution.py
@@ -15,6 +15,7 @@
 REACH = 6
 GREACH = 4
 WORDS = 5
+CHUNK = 10
 SIDE = 16
 PAD = 8
 DIRS = ((0, 1), (0, -1), (1, 0), (-1, 0), (1, 1), (1, -1), (-1, 1), (-1, -1))
@@ -243,19 +244,36 @@
             parts.append(ref[r // 2 : r // 2 + count // 2, r % 2].reshape(-1, 3 * chan))
         return jnp.concatenate(parts, axis=1)
 
-    def forward(s, m):
+    def chunked(multiply, finish, start, count, which):
+        before = None
+        for m in which:
+            for c in range(0, count, CHUNK):
+                now = (m, start + c, min(CHUNK, count - c))
+                product = multiply(*now)
+                if before:
+                    finish(*before)
+                before = (*now, product)
+        finish(*before)
+
+    def forward(s, which=range(MB)):
         start, count = (s + 1, tall - 2 * (s + 1)) if s < SEG - 1 else (REACH, rows)
-        y = jnp.dot(windows(aa.at[s, m], start, count), wf[s], preferred_element_type=F32)
-        for h in range(2):
-            i, par = (start + h) // 2, (start + h) % 2
-            n = count // 2
-            x = xs[m, i : i + n, par].astype(F32)
-            x = x + (y[:, h * chan : (h + 1) * chan].reshape(n, wp, chan) + ball[s][None])
-            x = jnp.where(in_image(start + h, 2, n), x, 0.0).astype(BF)
-            xs[m, i : i + n, par] = x
-            if s < SEG - 1:
-                for t, part in enumerate(trio(jnp.maximum(x.astype(F32), 0.0))):
-                    aa[s + 1, m, i : i + n, par, :, pl.ds(t * chan, chan)] = part
+
+        def multiply(m, first, n):
+            return jnp.dot(windows(aa.at[s, m], first, n), wf[s], preferred_element_type=F32)
+
+        def finish(m, first, n, y):
+            n = n // 2
+            for h in range(2):
+                i, par = (first + h) // 2, (first + h) % 2
+                x = xs[m, i : i + n, par].astype(F32)
+                x = x + (y[:, h * chan : (h + 1) * chan].reshape(n, wp, chan) + ball[s][None])
+                x = jnp.where(in_image(first + h, 2, n), x, 0.0).astype(BF)
+                xs[m, i : i + n, par] = x
+                if s < SEG - 1:
+                    for t, part in enumerate(trio(jnp.maximum(x.astype(F32), 0.0))):
+                        aa[s + 1, m, i : i + n, par, :, pl.ds(t * chan, chan)] = part
+
+        chunked(multiply, finish, start, count, which)
 
     def block_of(ref, m):
         lo, up_to = REACH // 2, hi // 2
@@ -283,22 +301,22 @@
     for copy in b_in:
         copy.wait_recv()
     build(0)
-    forward(0, 0)
+    forward(0, (0,))
     wait_in(1)
     take_in(1)
-    forward(0, 1)
+    forward(0, (1,))
     pass_word(2)
     pl.when(seg == 3)(pass_far)
     pl.when(seg == 0)(emit_x)
     need(1)
     build(1)
-    both(lambda m: forward(1, m))
+    forward(1)
     pass_word(3)
     pl.when(seg < 2)(pass_far)
     pl.when(seg == 1)(emit_x)
     need(2)
     build(2)
-    both(lambda m: forward(2, m))
+    forward(2)
     pass_word(4)
     pl.when(seg == 2)(emit_x)
     need(3)
@@ -328,26 +346,32 @@
 
         both(one)
 
-    def backward(k, m, slot, start, count, more):
-        y = lax.dot_general(
-            windows(gg.at[slot, m], start, count), wb[k], (((1,), (1,)), ((), ())),
-            preferred_element_type=F32,
-        )
-        for h in range(2):
-            i, par = (start + h) // 2, (start + h) % 2
-            n = count // 2
-            on = aa[k, m, i : i + n, par, :, pl.ds(chan, chan)].astype(F32) > 0.0
-            g = gs[m, i : i + n, par].astype(F32)
-            g = (g + jnp.where(on, y[:, h * chan : (h + 1) * chan].reshape(n, wp, chan), 0.0)).astype(BF)
-            gs[m, i : i + n, par] = g
-            if more:
-                for t, part in enumerate(trio(g.astype(F32))):
-                    gg[1 - slot, m, i : i + n, par, :, pl.ds(t * chan, chan)] = part
+    def backward(k, which, slot, start, count, more):
+        def multiply(m, first, n):
+            return lax.dot_general(
+                windows(gg.at[slot, m], first, n), wb[k], (((1,), (1,)), ((), ())),
+                preferred_element_type=F32,
+            )
+
+        def finish(m, first, n, y):
+            n = n // 2
+            for h in range(2):
+                i, par = (first + h) // 2, (first + h) % 2
+                on = aa[k, m, i : i + n, par, :, pl.ds(chan, chan)].astype(F32) > 0.0
+                g = gs[m, i : i + n, par].astype(F32)
+                y_h = y[:, h * chan : (h + 1) * chan].reshape(n, wp, chan)
+                g = (g + jnp.where(on, y_h, 0.0)).astype(BF)
+                gs[m, i : i + n, par] = g
+                if more:
+                    for t, part in enumerate(trio(g.astype(F32))):
+                        gg[1 - slot, m, i : i + n, par, :, pl.ds(t * chan, chan)] = part
+
+        chunked(multiply, finish, start, count, which)
 
     for k in range(SEG - 1, 0, -1):
 
         def stage(k=k):
-            both(lambda m: backward(k, m, k % 2, REACH - k, rows + 2 * k, True))
+            backward(k, range(MB), k % 2, REACH - k, rows + 2 * k, True)
 
         pl.when(seg < k)(stage)
         if k == SEG - 1:
@@ -355,10 +379,10 @@
     keep()
 
     def own_grad(m):
-        backward(seg, m, lax.rem(seg, 2), REACH, rows, False)
+        backward(seg, (m,), lax.rem(seg, 2), REACH, rows, False)
 
     def last_x():
-        both(lambda m: forward(SEG - 1, m))
+        forward(SEG - 1)
         emit_x()
 
     total = None

time: 48.1 us -> 46.4 us (0.965)
  Pallas kernels: 47.4 us -> 45.7 us
    pallas_call x1, Pallas kernels: 46.4 us -> 44.7 us  [body(): results = call(images, cotangent, weights.reshape(TAPS, chan, chan), biases)]
where the time goes in v4:
time: 46.4 us; the launch traced here: 46.3 us
  Pallas kernels  45.7 us (98%)
  between operations  0.64 us (1%)
    pallas_call x1, Pallas kernels, body(): results = call(images, cotangent, weights.reshape(TAPS, chan, chan), biases)  44.7 us
    pallas_call x1, Pallas kernels, body(): pl.pallas_call(write_kernel, out_shape=(jax.ShapeDtypeStruct(images.shape...  1.02 us

profile of v4, /device:TPU:1, one launch (start us, length us, event | category | flops | bytes accessed | tf_op | source)
XLA Modules:
  0.0 46.3 jit_solution(12767944812354223159)
XLA Ops:
  0.6 44.7 %shard_map.67 = (bf16[2,8,64,128]{3,2,1,0:T(8,128)(2,1)S(1)}, bf16[2,8,64,128]{3,2,1,0:T(8,128)(2,1)S(1)}, bf16[9,128,128]{2,1,0:T(8,128)(2,1)S(1)}) custom-call(bf16[2,8,64,128]{3,2,1,0:T(8,128)(2,1)} %images.1, bf16[2,8,64,128]{3,2,1,0:T(8,128)(2,1)} %cot.1, bf16[9,128,128]{2,1,0:T(8,128)(2,1)} %bitcast.4, f32[1,128]{1,0:T(1,128)} %b.1), custom_call_target="tpu_custom_call" | custom-call | tf_op jit(solution)/shard_map/pallas_call | solution.py:585
  45.3 1.0 %shard_map.68 = (bf16[2,8,64,128]{3,2,1,0:T(8,128)(2,1)}, bf16[2,8,64,128]{3,2,1,0:T(8,128)(2,1)}, f32[9,128,128]{2,1,0:T(8,128)}) custom-call(bf16[2,8,64,128]{3,2,1,0:T(8,128)(2,1)S(1)} %get-tuple-element.9.x, bf16[2,8,64,128]{3,2,1,0:T(8,128)(2,1)S(1)} %get-tuple-element.10.g, bf16[9,128,128]{2,1,0:T(8,128)(2,1)S(1)} %get-tuple-element.11.k), custom_call_target="tpu_custom_call" | custom-call | tf_op jit(solution)/shard_map/pallas_call | solution.py:586

commit v5 on v4

--- a/solution.py
+++ b/solution.py
@@ -27,7 +27,7 @@
 
 def body_kernel(
     dims, images, cot, w, b, ox, og, full,
-    xin, gin, wall, ball, aa, xs, gg, gs, gm, wf, wb,
+    xin, gin, wall, ball, aa, xs, gg, gs, gm, mask,
     dw, s_core, r_core, d_half, r_main, r_tap_col, s_tap, r_tap_row,
     ss, rs, ls, words,
 ):
@@ -171,9 +171,9 @@
         b_out.append(remote(b, ball.at[seg], (lax.rem(seg + k, SEG), row, col), i))
         b_in.append(remote(b, ball.at[lax.rem(seg + SEG - k, SEG)], (lax.rem(seg + k, SEG), row, col), i))
 
+    for copy in w_out:
+        copy.start()
     start_edges(x_edges[0])
-    for copy in w_out:
-        copy.start()
     start_edges(x_edges[1])
     for copy in b_out:
         copy.start()
@@ -206,6 +206,8 @@
         c = col * width - PAD + lax.broadcasted_iota(jnp.int32, shape, 1)
         return (r >= 0) & (r < nrow * rows) & (c >= 0) & (c < ncol * width)
 
+    mask[...] = jnp.where(in_image(0, 1, tall), 1.0, 0.0).reshape(mask.shape)
+
     def trio(value):
         flat = value.reshape(-1, chan)
         n = flat.shape[0]
@@ -216,7 +218,7 @@
 
     def take_in(m):
         v = xin[m].astype(F32)[:, PAD : PAD + wp]
-        v = jnp.where(in_image(0, 1, tall), v, 0.0)
+        v = jnp.where(mask[...].reshape(tall, wp, chan) > 0.0, v, 0.0)
         xs[m] = v.astype(BF).reshape(tall // 2, 2, wp, chan)
         for t, part in enumerate(trio(jnp.maximum(v, 0.0))):
             aa[0, m, :, :, :, pl.ds(t * chan, chan)] = part.reshape(tall // 2, 2, wp, chan)
@@ -225,17 +227,24 @@
         mine[m].wait()
         wait_edges(x_edges[m])
 
-    def build(k):
-        zero = jnp.zeros((3 * chan, chan), BF)
-        for a in range(4):
-            for h in range(2):
-                ok = 0 <= a - h <= 2
-                block = wall[k, 3 * (a - h) : 3 * (a - h) + 3].reshape(3 * chan, chan) if ok else zero
-                wf[k, pl.ds(a * 3 * chan, 3 * chan), pl.ds(h * chan, chan)] = block
-                for t in range(3):
-                    p = h + 2 - a
-                    tile = wall[k, 3 * p + 2 - t] if 0 <= p <= 2 else zero[:chan]
-                    wb[k, pl.ds(h * chan, chan), pl.ds((3 * a + t) * chan, chan)] = tile
+    zero = jnp.zeros((chan, chan), BF)
+
+    def tile(k, p, q):
+        return wall[k, 3 * p + q] if 0 <= p <= 2 else zero
+
+    def there(k):
+        rows_of = [
+            jnp.concatenate([tile(k, a, t), tile(k, a - 1, t)], axis=1)
+            for a in range(4) for t in range(3)
+        ]
+        return jnp.concatenate(rows_of, axis=0)
+
+    def back(k):
+        rows_of = [
+            jnp.concatenate([tile(k, h + 2 - a, 2 - t) for a in range(4) for t in range(3)], axis=1)
+            for h in range(2)
+        ]
+        return jnp.concatenate(rows_of, axis=0)
 
     def windows(ref, start, count):
         parts = []
@@ -259,7 +268,7 @@
         start, count = (s + 1, tall - 2 * (s + 1)) if s < SEG - 1 else (REACH, rows)
 
         def multiply(m, first, n):
-            return jnp.dot(windows(aa.at[s, m], first, n), wf[s], preferred_element_type=F32)
+            return jnp.dot(windows(aa.at[s, m], first, n), there(s), preferred_element_type=F32)
 
         def finish(m, first, n, y):
             n = n // 2
@@ -267,7 +276,7 @@
                 i, par = (first + h) // 2, (first + h) % 2
                 x = xs[m, i : i + n, par].astype(F32)
                 x = x + (y[:, h * chan : (h + 1) * chan].reshape(n, wp, chan) + ball[s][None])
-                x = jnp.where(in_image(first + h, 2, n), x, 0.0).astype(BF)
+                x = jnp.where(mask[i : i + n, par] > 0.0, x, 0.0).astype(BF)
                 xs[m, i : i + n, par] = x
                 if s < SEG - 1:
                     for t, part in enumerate(trio(jnp.maximum(x.astype(F32), 0.0))):
@@ -300,7 +309,6 @@
     mine_b.wait()
     for copy in b_in:
         copy.wait_recv()
-    build(0)
     forward(0, (0,))
     wait_in(1)
     take_in(1)
@@ -309,26 +317,18 @@
     pl.when(seg == 3)(pass_far)
     pl.when(seg == 0)(emit_x)
     need(1)
-    build(1)
     forward(1)
     pass_word(3)
     pl.when(seg < 2)(pass_far)
     pl.when(seg == 1)(emit_x)
-    need(2)
-    build(2)
-    forward(2)
-    pass_word(4)
-    pl.when(seg == 2)(emit_x)
-    need(3)
-    build(3)
-
     mine_g.wait()
     wait_edges(g_edges)
     edge = REACH - GREACH
+
     def take_in_grad(m):
         v = gin[m].astype(F32)[:, PAD : PAD + wp]
-        v = jnp.where(in_image(edge, 1, tall - 2 * edge), v, 0.0)
         lo, n = edge // 2, tall // 2 - edge
+        v = jnp.where(mask[lo : lo + n].reshape(v.shape) > 0.0, v, 0.0)
         gs[m, lo : lo + n] = v.astype(BF).reshape(n, 2, wp, chan)
         for t, part in enumerate(trio(v)):
             gg[1, m, lo : lo + n, :, :, pl.ds(t * chan, chan)] = part.reshape(n, 2, wp, chan)
@@ -337,6 +337,11 @@
         gm[m, rows + 2 : rows + 4] = nothing
 
     both(take_in_grad)
+    need(2)
+    forward(2)
+    pass_word(4)
+    pl.when(seg == 2)(emit_x)
+    need(3)
 
     def keep():
         c = lax.broadcasted_iota(jnp.int32, (rows, wp, chan), 1)
@@ -349,7 +354,7 @@
     def backward(k, which, slot, start, count, more):
         def multiply(m, first, n):
             return lax.dot_general(
-                windows(gg.at[slot, m], first, n), wb[k], (((1,), (1,)), ((), ())),
+                windows(gg.at[slot, m], first, n), back(k), (((1,), (1,)), ((), ())),
                 preferred_element_type=F32,
             )
 
@@ -563,8 +568,7 @@
             vm((2, MB, tall // 2, 2, wp, 3 * chan), BF),
             vm((MB, tall // 2, 2, wp, chan), BF),
             vm((MB, rows + 4, wp, chan), BF),
-            vm((SEG, 12 * chan, 2 * chan), BF),
-            vm((SEG, 2 * chan, 12 * chan), BF),
+            vm((tall // 2, 2, wp, chan), F32),
             vm((TAPS, chan, chan), F32),
             vm((TAPS, half, chan), BF),
             vm((TAPS, half, chan), BF),

time: 46.4 us -> 45.4 us (0.978)
  Pallas kernels: 45.7 us -> 44.7 us
    pallas_call x1, Pallas kernels: 44.7 us -> 43.7 us  [body(): results = call(images, cotangent, weights.reshape(TAPS, chan, chan), biases)]
where the time goes in v5:
time: 45.4 us; the launch traced here: 45.3 us
  Pallas kernels  44.7 us (98%)
  between operations  0.64 us (1%)
    pallas_call x1, Pallas kernels, body(): results = call(images, cotangent, weights.reshape(TAPS, chan, chan), biases)  43.7 us
    pallas_call x1, Pallas kernels, body(): pl.pallas_call(write_kernel, out_shape=(jax.ShapeDtypeStruct(images.shape...  1.02 us

profile of v5, /device:TPU:1, one launch (start us, length us, event | category | flops | bytes accessed | tf_op | source)
XLA Modules:
  0.0 45.3 jit_solution(1163319444897782392)
XLA Ops:
  0.6 43.7 %shard_map.67 = (bf16[2,8,64,128]{3,2,1,0:T(8,128)(2,1)S(1)}, bf16[2,8,64,128]{3,2,1,0:T(8,128)(2,1)S(1)}, bf16[9,128,128]{2,1,0:T(8,128)(2,1)S(1)}) custom-call(bf16[2,8,64,128]{3,2,1,0:T(8,128)(2,1)} %images.1, bf16[2,8,64,128]{3,2,1,0:T(8,128)(2,1)} %cot.1, bf16[9,128,128]{2,1,0:T(8,128)(2,1)} %bitcast.4, f32[1,128]{1,0:T(1,128)} %b.1), custom_call_target="tpu_custom_call" | custom-call | tf_op jit(solution)/shard_map/pallas_call | solution.py:589
  44.3 1.0 %shard_map.68 = (bf16[2,8,64,128]{3,2,1,0:T(8,128)(2,1)}, bf16[2,8,64,128]{3,2,1,0:T(8,128)(2,1)}, f32[9,128,128]{2,1,0:T(8,128)}) custom-call(bf16[2,8,64,128]{3,2,1,0:T(8,128)(2,1)S(1)} %get-tuple-element.9.x, bf16[2,8,64,128]{3,2,1,0:T(8,128)(2,1)S(1)} %get-tuple-element.10.g, bf16[9,128,128]{2,1,0:T(8,128)(2,1)S(1)} %get-tuple-element.11.k), custom_call_target="tpu_custom_call" | custom-call | tf_op jit(solution)/shard_map/pallas_call | solution.py:590

commit v6 on v5

--- a/solution.py
+++ b/solution.py
@@ -18,7 +18,7 @@
 CHUNK = 10
 SIDE = 16
 PAD = 8
-DIRS = ((0, 1), (0, -1), (1, 0), (-1, 0), (1, 1), (1, -1), (-1, 1), (-1, -1))
+DIRS = ((1, 1), (1, -1), (-1, 1), (-1, -1), (1, 0), (-1, 0), (0, 1), (0, -1))
 
 
 def wrap(v, n):
@@ -56,6 +56,33 @@
             device_id=dev, device_id_type=MESH,
         )
 
+    barrier = pltpu.get_barrier_semaphore()
+
+    def greet(s, r, c):
+        pl.semaphore_signal(barrier, inc=1, device_id=(s, r, c), device_id_type=MESH)
+
+    def inside(dr, dc):
+        ok = jnp.bool_(True)
+        if dr:
+            ok = ok & (row + dr >= 0) & (row + dr < nrow)
+        if dc:
+            ok = ok & (col + dc >= 0) & (col + dc < ncol)
+        return ok
+
+    met = SEG - 1 + 4
+    for dr, dc in DIRS:
+        if dr:
+            pl.when(inside(dr, dc))(functools.partial(greet, seg, row + dr, col + dc))
+            met = met + inside(dr, dc).astype(jnp.int32)
+    for k in range(1, SEG):
+        greet(lax.rem(seg + k, SEG), row, col)
+    beside_z = [lax.rem(row + 2, nrow), lax.rem(row + nrow - 2, nrow)]
+    beside_y = [lax.rem(col + 1, ncol), lax.rem(col + ncol - 1, ncol)]
+    for r in beside_z:
+        greet(seg, r, col)
+    for c in beside_y:
+        greet(seg, row, c)
+
     mine = [
         pltpu.make_async_copy(images.at[m], xin.at[m, pl.ds(REACH, rows), pl.ds(SIDE, width)], ls.at[m])
         for m in range(MB)
@@ -66,32 +93,6 @@
     for copy in (*mine, mine_g, mine_w, mine_b):
         copy.start()
 
-    barrier = pltpu.get_barrier_semaphore()
-
-    def greet(s, r, c):
-        pl.semaphore_signal(barrier, inc=1, device_id=(s, r, c), device_id_type=MESH)
-
-    def inside(dr, dc):
-        ok = jnp.bool_(True)
-        if dr:
-            ok = ok & (row + dr >= 0) & (row + dr < nrow)
-        if dc:
-            ok = ok & (col + dc >= 0) & (col + dc < ncol)
-        return ok
-
-    for k in range(1, SEG):
-        greet(lax.rem(seg + k, SEG), row, col)
-    beside_z = [lax.rem(row + 2, nrow), lax.rem(row + nrow - 2, nrow)]
-    beside_y = [lax.rem(col + 1, ncol), lax.rem(col + ncol - 1, ncol)]
-    for r in beside_z:
-        greet(seg, r, col)
-    for c in beside_y:
-        greet(seg, row, c)
-    met = SEG - 1 + 4
-    for dr, dc in DIRS:
-        if dr:
-            pl.when(inside(dr, dc))(functools.partial(greet, seg, row + dr, col + dc))
-            met = met + inside(dr, dc).astype(jnp.int32)
     pl.semaphore_wait(barrier, met)
 
     def pass_word(n):
@@ -128,7 +129,7 @@
             pl.when(to)(copy.start)
 
     def wait_edges(copies):
-        for copy, _, of in copies:
+        for copy, _, of in reversed(copies):
             pl.when(of)(copy.wait_recv)
 
     x_edges = [
@@ -174,9 +175,9 @@
     for copy in w_out:
         copy.start()
     start_edges(x_edges[0])
+    for copy in b_out:
+        copy.start()
     start_edges(x_edges[1])
-    for copy in b_out:
-        copy.start()
     start_edges(g_edges)
 
     def pass_near():
@@ -486,7 +487,7 @@
             remote(src, src, device(ky, kz), i),
             remote(src, full.at[taps[-kz % nz], places[-ky % ncol]], device(ky, kz), i),
         ))
-    for _, copy in sums:
+    for _, copy in reversed(sums):
         copy.wait_recv()
     full[taps[0], places[0]] = (total_of(r_main, ncol * nz) * scale).astype(BF)
     for copy, _ in spread:
@@ -515,7 +516,7 @@
     for copy in (core_sum, *tap_col):
         copy.wait_send()
 
-    for _, copy in (*spread, *tap_all):
+    for _, copy in (*reversed(spread), *tap_all):
         copy.wait_recv()
     i = fresh()
     core_all = remote(full.at[:, own_rows], full.at[:, own_rows], beside, i)

time: 45.4 us -> 45 us (level)
  no operation moved by 1% of the time
where the time goes in v6:
time: 45 us; the launch traced here: 44.9 us
  Pallas kernels  44.3 us (98%)
  between operations  0.64 us (1%)
    pallas_call x1, Pallas kernels, body(): results = call(images, cotangent, weights.reshape(TAPS, chan, chan), biases)  43.3 us
    pallas_call x1, Pallas kernels, body(): pl.pallas_call(write_kernel, out_shape=(jax.ShapeDtypeStruct(images.shape...  1.02 us

profile of v6, /device:TPU:1, one launch (start us, length us, event | category | flops | bytes accessed | tf_op | source)
XLA Modules:
  0.0 44.9 jit_solution(8956062569336601591)
XLA Ops:
  0.6 43.3 %shard_map.67 = (bf16[2,8,64,128]{3,2,1,0:T(8,128)(2,1)S(1)}, bf16[2,8,64,128]{3,2,1,0:T(8,128)(2,1)S(1)}, bf16[9,128,128]{2,1,0:T(8,128)(2,1)S(1)}) custom-call(bf16[2,8,64,128]{3,2,1,0:T(8,128)(2,1)} %images.1, bf16[2,8,64,128]{3,2,1,0:T(8,128)(2,1)} %cot.1, bf16[9,128,128]{2,1,0:T(8,128)(2,1)} %bitcast.4, f32[1,128]{1,0:T(1,128)} %b.1), custom_call_target="tpu_custom_call" | custom-call | tf_op jit(solution)/shard_map/pallas_call | solution.py:590
  43.9 1.0 %shard_map.68 = (bf16[2,8,64,128]{3,2,1,0:T(8,128)(2,1)}, bf16[2,8,64,128]{3,2,1,0:T(8,128)(2,1)}, f32[9,128,128]{2,1,0:T(8,128)}) custom-call(bf16[2,8,64,128]{3,2,1,0:T(8,128)(2,1)S(1)} %get-tuple-element.9.x, bf16[2,8,64,128]{3,2,1,0:T(8,128)(2,1)S(1)} %get-tuple-element.10.g, bf16[9,128,128]{2,1,0:T(8,128)(2,1)S(1)} %get-tuple-element.11.k), custom_call_target="tpu_custom_call" | custom-call | tf_op jit(solution)/shard_map/pallas_call | solution.py:591

commit v7 on v6

--- a/solution.py
+++ b/solution.py
@@ -180,11 +180,13 @@
     start_edges(x_edges[1])
     start_edges(g_edges)
 
-    def pass_near():
+    def relay():
         got_prv[0].wait_recv()
         relay_up.start()
         got_nxt[0].wait_recv()
         relay_down.start()
+
+    def pass_near():
         got_prv[1].wait_recv()
         share_prv.start()
         got_nxt[1].wait_recv()
@@ -301,6 +303,7 @@
 
         both(one)
 
+    relay()
     wait_in(0)
     take_in(0)
     pass_near()

time: 45 us -> 45.4 us (level)
  no operation moved by 1% of the time
where the time goes in v7:
time: 45.4 us; the launch traced here: 45.3 us
  Pallas kernels  44.7 us (98%)
  between operations  0.64 us (1%)
    pallas_call x1, Pallas kernels, body(): results = call(images, cotangent, weights.reshape(TAPS, chan, chan), biases)  43.7 us
    pallas_call x1, Pallas kernels, body(): pl.pallas_call(write_kernel, out_shape=(jax.ShapeDtypeStruct(images.shape...  1.02 us

profile of v7, /device:TPU:1, one launch (start us, length us, event | category | flops | bytes accessed | tf_op | source)
XLA Modules:
  0.0 45.3 jit_solution(3853075434196709115)
XLA Ops:
  0.6 43.7 %shard_map.67 = (bf16[2,8,64,128]{3,2,1,0:T(8,128)(2,1)S(1)}, bf16[2,8,64,128]{3,2,1,0:T(8,128)(2,1)S(1)}, bf16[9,128,128]{2,1,0:T(8,128)(2,1)S(1)}) custom-call(bf16[2,8,64,128]{3,2,1,0:T(8,128)(2,1)} %images.1, bf16[2,8,64,128]{3,2,1,0:T(8,128)(2,1)} %cot.1, bf16[9,128,128]{2,1,0:T(8,128)(2,1)} %bitcast.4, f32[1,128]{1,0:T(1,128)} %b.1), custom_call_target="tpu_custom_call" | custom-call | tf_op jit(solution)/shard_map/pallas_call | solution.py:593
  44.3 1.0 %shard_map.68 = (bf16[2,8,64,128]{3,2,1,0:T(8,128)(2,1)}, bf16[2,8,64,128]{3,2,1,0:T(8,128)(2,1)}, f32[9,128,128]{2,1,0:T(8,128)}) custom-call(bf16[2,8,64,128]{3,2,1,0:T(8,128)(2,1)S(1)} %get-tuple-element.9.x, bf16[2,8,64,128]{3,2,1,0:T(8,128)(2,1)S(1)} %get-tuple-element.10.g, bf16[9,128,128]{2,1,0:T(8,128)(2,1)S(1)} %get-tuple-element.11.k), custom_call_target="tpu_custom_call" | custom-call | tf_op jit(solution)/shard_map/pallas_call | solution.py:594
